TPU v7x, 512 devices: a whole 4x4x16 slice. The times are simulated.
512 devices in a mesh: lat: 16 (over y_hi, x, core), lon: 32 (over y_lo, z).
Axes of the slice: x: 4, y: 4 (y_hi: 2, y_lo: 2; y = y_hi * 2 + y_lo), z: 16, core: 2. Of those that a mesh axis runs over, the one named last changes fastest.
Arguments:
- tokens: bfloat16 [288, 768, 512], P('lat', 'lon'), may hold values from -6 to 6
- grad_output: bfloat16 [288, 768, 512], P('lat', 'lon'), may hold values from -6 to 6
- qkv_weight: bfloat16 [512, 1536], P('lat'), may hold values from -2 to 2
- proj_weight: bfloat16 [512, 512], P('lat'), may hold values from -0.25 to 0.25
- expand_weight: bfloat16 [512, 2048], P('lat'), may hold values from -0.25 to 0.25
- contract_weight: bfloat16 [2048, 512], P('lat'), may hold values from -0.125 to 0.125
Outputs:
- output: bfloat16 [288, 768, 512], P('lat', 'lon')
- grad_tokens: bfloat16 [288, 768, 512], P('lat', 'lon')
All inputs are finite; a program needn't handle non-finite values.
Results may differ from a plain program's by a relative error of at most 0.009.
Values may be sent and summed in bfloat16 or wider, within the bound.
A program may use at most 64 MiB of HBM per device.

v0:
```python
import jax
import jax.numpy as jnp
from jax import lax
from jax.sharding import PartitionSpec as P

HEADS = 8
WIN_LAT = 6
WIN_LON = 12


EPSILON = 1e-05


def shifted_2(value, axis, steps):
    count = lax.axis_size(axis)
    pairs = [(source, (source + steps) % count) for source in range(count)]
    return lax.ppermute(value, axis, pairs)


def product(pattern, operand, other):
    return jnp.einsum(pattern, operand, other, preferred_element_type=jnp.float32)


def normalize(values):
    average = jnp.mean(values, axis=-1, keepdims=True)
    centred = values - average
    inverse = lax.rsqrt(jnp.mean(centred * centred, axis=-1, keepdims=True) + EPSILON)
    return (centred * inverse, inverse)


def normalize_back(scaled, inverse, gradient):
    mean_grad = jnp.mean(gradient, axis=-1, keepdims=True)
    projected = jnp.mean(gradient * scaled, axis=-1, keepdims=True)
    return inverse * (gradient - mean_grad - scaled * projected)


def gelu_value(preact):
    return 0.5 * preact * (1.0 + lax.erf(preact * 0.7071067811865476))


def gelu_slope(preact):
    return (
        0.5 * (1.0 + lax.erf(preact * 0.7071067811865476))
        + preact * jnp.exp(-0.5 * preact * preact) * 0.3989422804014327
    )


def split_windows(grid):
    height, breadth, channels = grid.shape
    blocks = grid.reshape(height // WIN_LAT, WIN_LAT, breadth // WIN_LON, WIN_LON, channels)
    blocks = jnp.transpose(blocks, (0, 2, 1, 3, 4))
    return blocks.reshape(height // WIN_LAT * (breadth // WIN_LON), WIN_LAT * WIN_LON, channels)


def join_windows(blocks, height, breadth):
    channels = blocks.shape[-1]
    grid = blocks.reshape(height // WIN_LAT, breadth // WIN_LON, WIN_LAT, WIN_LON, channels)
    grid = jnp.transpose(grid, (0, 2, 1, 3, 4))
    return grid.reshape(height, breadth, channels)


def assemble(tile):
    shift_lat = WIN_LAT // 2
    shift_lon = WIN_LON // 2
    rows_rim = shifted_2(tile[:shift_lat], "lat", -1)
    taller = jnp.concatenate([tile, rows_rim], axis=0)
    cols_rim = shifted_2(taller[:, :shift_lon], "lon", -1)
    wider = jnp.concatenate([taller, cols_rim], axis=1)
    return wider[shift_lat:, shift_lon:]


def disperse(shifted):
    shift_lat = WIN_LAT // 2
    shift_lon = WIN_LON // 2
    height, breadth, channels = shifted.shape
    cols_rim = shifted_2(shifted[:, breadth - shift_lon :], "lon", 1)
    fixed = jnp.concatenate([cols_rim, shifted], axis=1)[:, :breadth]
    rows_rim = shifted_2(fixed[height - shift_lat :], "lat", 1)
    return jnp.concatenate([rows_rim, fixed], axis=0)[:height]


def attend_parts(windows, labels, qkv_weight):
    window_count, length, channels = windows.shape
    head_size = channels // HEADS
    proj = product("blc,cd->bld", windows, qkv_weight).astype(jnp.bfloat16)
    proj = proj.reshape(window_count, length, 3, HEADS, head_size)
    query_part, key_part, value_part = (proj[:, :, 0], proj[:, :, 1], proj[:, :, 2])
    scores = product("bqhd,bkhd->bhqk", query_part, key_part) * head_size ** (-0.5)
    allowed = (labels[:, :, None] == labels[:, None, :])[:, None]
    scores = jnp.where(allowed, scores, -1e30)
    largest = jnp.max(scores, axis=-1, keepdims=True)
    exponent = jnp.exp(scores - largest)
    softmax_out = exponent / jnp.sum(exponent, axis=-1, keepdims=True)
    return (query_part, key_part, value_part, softmax_out)


def attend_forward(parts, proj_weight):
    query_part, key_part, value_part, softmax_out = parts
    window_count, length, heads_here, head_size = query_part.shape
    mixed = product("bhqk,bkhd->bqhd", softmax_out.astype(jnp.bfloat16), value_part).astype(
        jnp.bfloat16
    )
    mixed = mixed.reshape(window_count, length, heads_here * head_size)
    return product("blc,cd->bld", mixed, proj_weight).astype(jnp.bfloat16)


def attend_back(parts, grad_out, qkv_weight, proj_weight):
    query_part, key_part, value_part, softmax_out = parts
    window_count, length, heads_here, head_size = query_part.shape
    grad_mixed = product("bld,cd->blc", grad_out, proj_weight).astype(jnp.bfloat16)
    grad_mixed = grad_mixed.reshape(window_count, length, heads_here, head_size)
    grad_probs = product("bqhd,bkhd->bhqk", grad_mixed, value_part)
    grad_values = product("bhqk,bqhd->bkhd", softmax_out.astype(jnp.bfloat16), grad_mixed).astype(
        jnp.bfloat16
    )
    grad_scores = softmax_out * (
        grad_probs - jnp.sum(grad_probs * softmax_out, axis=-1, keepdims=True)
    )
    grad_scores = (grad_scores * head_size ** (-0.5)).astype(jnp.bfloat16)
    grad_queries = product("bhqk,bkhd->bqhd", grad_scores, key_part).astype(jnp.bfloat16)
    grad_keys = product("bhqk,bqhd->bkhd", grad_scores, query_part).astype(jnp.bfloat16)
    grad_proj = jnp.stack([grad_queries, grad_keys, grad_values], axis=2)
    grad_proj = grad_proj.reshape(window_count, length, 3 * heads_here * head_size)
    return product("bld,cd->blc", grad_proj, qkv_weight).astype(jnp.bfloat16)


def shards(tokens, grad_output, qkv_weight, proj_weight, expand_weight, contract_weight):
    height, breadth, channels = tokens.shape
    shift_lat = WIN_LAT // 2
    qkv_whole, proj_whole, expand_whole, contract_whole = (
        lax.all_gather(qkv_weight, "lat", axis=0, tiled=True),
        lax.all_gather(proj_weight, "lat", axis=0, tiled=True),
        lax.all_gather(expand_weight, "lat", axis=0, tiled=True),
        lax.all_gather(contract_weight, "lat", axis=0, tiled=True),
    )
    values32 = tokens.astype(jnp.float32)
    scaled1, inverse1 = normalize(values32)
    normal1 = scaled1.astype(jnp.bfloat16)
    shifted = assemble(normal1)
    total_rows = height * lax.axis_size("lat")
    global_row = lax.axis_index("lat") * height + jnp.arange(height, dtype=jnp.int32)
    row_label = (global_row >= total_rows - shift_lat).astype(jnp.int32)
    labels = jnp.broadcast_to(row_label[:, None, None], (height, breadth, 1))
    windows = split_windows(shifted)
    label_win = split_windows(labels)[..., 0]
    parts = attend_parts(windows, label_win, qkv_whole)
    attended = attend_forward(parts, proj_whole)
    attn = disperse(join_windows(attended, height, breadth))
    hidden = (values32 + attn.astype(jnp.float32)).reshape(height * breadth, channels)
    scaled2, inverse2 = normalize(hidden)
    normal2 = scaled2.astype(jnp.bfloat16)
    token_count = height * breadth
    preact = product("nc,cf->nf", normal2, expand_whole)
    activated = gelu_value(preact).astype(jnp.bfloat16)
    feed_out = product("nf,fc->nc", activated, contract_whole)
    output = (hidden + feed_out).astype(jnp.bfloat16).reshape(height, breadth, channels)
    flat_grad = grad_output.reshape(token_count, channels)
    grad_act = product("nc,fc->nf", flat_grad, contract_whole)
    grad_pre = (grad_act * gelu_slope(preact)).astype(jnp.bfloat16)
    grad_norm2 = product("nf,cf->nc", grad_pre, expand_whole)
    grad_hidden = flat_grad.astype(jnp.float32) + normalize_back(scaled2, inverse2, grad_norm2)
    grad_hidden = grad_hidden.reshape(height, breadth, channels)
    grad_attn = assemble(grad_hidden.astype(jnp.bfloat16))
    grad_shifted = attend_back(parts, split_windows(grad_attn), qkv_whole, proj_whole)
    grad_normal1 = disperse(join_windows(grad_shifted, height, breadth))
    grad_tokens = grad_hidden + normalize_back(scaled1, inverse1, grad_normal1.astype(jnp.float32))
    return (output, grad_tokens.astype(jnp.bfloat16))


def solution(mesh):
    return jax.shard_map(
        shards,
        mesh=mesh,
        in_specs=(
            P("lat", "lon", None),
            P("lat", "lon", None),
            P("lat", None),
            P("lat", None),
            P("lat", None),
            P("lat", None),
        ),
        out_specs=(P("lat", "lon", None), P("lat", "lon", None)),
        check_vma=False,
    )
```

profile of v0, /device:TPU:24, one launch (start us, length us, event | category | flops | bytes accessed | tf_op | source)
XLA Modules:
  0.0 306.5 jit_solution(17668816585575566306)
XLA Ops:
  12.4 4.8 %collective-permute-start = (bf16[3,24,512]{2,1,0:T(8,128)(2,1)S(1)}, bf16[3,24,512]{2,1,0:T(8,128)(2,1)S(1)}, u32[]{:S(2)}, u32[]{:S(2)}) collective-permute-start(bf16[3,24,512]{2,1,0:T(8,128)(2,1)S(1)} %slice.70), channel_id=1, source_target_pairs={{0,480},{32,0},{64,32},{96,64},{128,96},{160,128},{192,160},{224,1... | collective-permute-start | bytes 221192 | tf_op jit(solution)/shard_map/ppermute | solution.py:17
  17.2 21.2 %all_gather.13 = bf16[512,512]{1,0:T(8,128)(2,1)S(1)} all-gather(bf16[32,512]{1,0:T(8,128)(2,1)S(1)} %copy-done.6), channel_id=1, replica_groups=mesh['lat'=16,'lon'=32] {'lat'}, dimensions={0}, use_global_device_ids=true | all-gather | bytes 557056 | tf_op jit(solution)/shard_map/all_gather | solution.py:132
  38.6 10.9 %collective-permute-start.1 = (bf16[21,6,512]{2,1,0:T(8,128)(2,1)S(1)}, bf16[21,6,512]{2,1,0:T(8,128)(2,1)S(1)}, u32[]{:S(2)}, u32[]{:S(2)}) collective-permute-start(bf16[21,6,512]{2,1,0:T(8,128)(2,1)S(1)} %pad_maximum_fusion.10), channel_id=1, source_target_pairs={{0,31},{1,0},{2,1},{3,2},{4,3},{5,4},{6,5},{7,6},{8,7},{9,8},{10,9... | collective-permute-start | bytes 387080 | tf_op jit(solution)/shard_map/ppermute | solution.py:17
  50.2 3.4 %collective-permute-done.1 = bf16[21,6,512]{2,1,0:T(8,128)(2,1)S(1)} collective-permute-done((bf16[21,6,512]{2,1,0:T(8,128)(2,1)S(1)}, bf16[21,6,512]{2,1,0:T(8,128)(2,1)S(1)}, u32[]{:S(2)}, u32[]{:S(2)}) %collective-permute-start.1) | collective-permute-done | bytes 129056 | tf_op jit(solution)/shard_map/ppermute | solution.py:17
  54.0 22.1 %all-gather.4.cloned.1.call-done = bf16[512,1536]{1,0:T(8,128)(2,1)} async-done(((bf16[32,1536]{1,0:T(8,128)(2,1)}), bf16[512,1536]{1,0:T(8,128)(2,1)}) %all-gather.4.cloned.1.call-update) | async-done | bytes 1572880 | tf_op jit(solution)/shard_map/all_gather | solution.py:131
  76.2 3.3 %convolution_convert_fusion = bf16[6,72,1536]{2,1,0:T(8,128)(2,1)} fusion(bf16[6,72,512]{2,1,0:T(8,128)(2,1)S(1)} %reshape.131, bf16[512,1536]{1,0:T(8,128)(2,1)} %all-gather.4.cloned.1.call-done), kind=kOutput, calls=%fused_computation.11 | convolution fusion | flops 680140800 | bytes 3342336 | tf_op jit(solution)/shard_map/blc,cd->bld/dot_general | solution.py:21
  89.6 3.3 %fusion.98 = (f32[6,8,72]{2,1,0:T(8,128)S(1)}, f32[6,8,72,72]{2,3,1,0:T(8,128)}) fusion(pred[6,72,72]{1,2,0:T(8,128)(4,1)S(1)} %copy-done.5, bf16[6,72,1,8,64]{1,4,3,0,2:T(8,128)(2,1)} %copy.45, bf16[6,72,1,8,64]{1,4,3,0,2:T(8,128)(2,1)S(1)} %copy.44), kind=kOutput, calls=%fused_computation.116 | convolution fusion | flops 32845896 | bytes 1924992 | tf_op jit(solution)/shard_map/sub | solution.py:92
  97.5 3.5 %collective-permute-start.2 = (bf16[18,6,512]{2,1,0:T(8,128)(2,1)S(1)}, bf16[18,6,512]{2,1,0:T(8,128)(2,1)S(1)}, u32[]{:S(2)}, u32[]{:S(2)}) collective-permute-start(bf16[18,6,512]{2,1,0:T(8,128)(2,1)S(1)} %slice.74), channel_id=1, source_target_pairs={{0,1},{1,2},{2,3},{3,4},{4,5},{5,6},{6,7},{7,8},{8,9},{9,10},{10,1... | collective-permute-start | bytes 331784 | tf_op jit(solution)/shard_map/ppermute | solution.py:17
  101.0 6.5 %collective-permute-done.2 = bf16[18,6,512]{2,1,0:T(8,128)(2,1)S(1)} collective-permute-done((bf16[18,6,512]{2,1,0:T(8,128)(2,1)S(1)}, bf16[18,6,512]{2,1,0:T(8,128)(2,1)S(1)}, u32[]{:S(2)}, u32[]{:S(2)}) %collective-permute-start.2) | collective-permute-done | bytes 110624 | tf_op jit(solution)/shard_map/ppermute | solution.py:17
  109.5 7.4 %collective-permute-done.3 = bf16[3,24,512]{2,1,0:T(8,128)(2,1)S(1)} collective-permute-done((bf16[3,24,512]{2,1,0:T(8,128)(2,1)S(1)}, bf16[3,24,512]{2,1,0:T(8,128)(2,1)S(1)}, u32[]{:S(2)}, u32[]{:S(2)}) %collective-permute-start.3) | collective-permute-done | bytes 73760 | tf_op jit(solution)/shard_map/ppermute | solution.py:17
  117.7 24.4 %all-gather.6.cloned.1.call-done = bf16[512,2048]{1,0:T(8,128)(2,1)} async-done(((bf16[32,2048]{1,0:T(8,128)(2,1)}), bf16[512,2048]{1,0:T(8,128)(2,1)}) %all-gather.6.cloned.1.call-update) | async-done | bytes 2097168 | tf_op jit(solution)/shard_map/all_gather | solution.py:133
  142.2 4.5 %fusion.68 = f32[432,2048]{1,0:T(8,128)} fusion(bf16[512,2048]{1,0:T(8,128)(2,1)} %all-gather.6.cloned.1.call-done, f32[432,512]{1,0:T(8,128)S(1)} %fusion.52), kind=kOutput, calls=%fused_computation.84 | convolution fusion | flops 906190848 | bytes 6520832 | tf_op jit(solution)/shard_map/nc,cf->nf/dot_general | solution.py:21
  146.6 61.6 %all-gather.8.cloned.1.call-done = bf16[2048,512]{1,0:T(8,128)(2,1)} async-done(((bf16[128,512]{1,0:T(8,128)(2,1)}), bf16[2048,512]{1,0:T(8,128)(2,1)}) %all-gather.8.cloned.1.call-update) | async-done | bytes 2097168 | tf_op jit(solution)/shard_map/all_gather | solution.py:134
  208.3 7.4 %fusion.95 = (f32[432]{0:T(512)}, f32[432]{0:T(512)}, f32[432,512]{1,0:T(8,128)}) fusion(f32[432,512]{1,0:T(8,128)S(1)} %fusion.52, bf16[512,2048]{1,0:T(8,128)(2,1)} %all-gather.6.cloned.1.call-done, f32[432,2048]{1,0:T(8,128)} %fusion.68, bf16[432,512]{1,0:T(8,128)(2,1)} %bitcast.96, bf16[2048,512]{1,0:T(8,128)(2,1)} %all-gather.8.cloned.1.call-done), kind=kOutput, calls=%fused_computation.113 | convolution fusion | flops 1821449472 | bytes 9948544 | tf_op jit(solution)/shard_map/nf,cf->nc/dot_general | solution.py:21
  218.1 5.7 %collective-permute-start.4 = (bf16[3,24,512]{2,1,0:T(8,128)(2,1)S(1)}, bf16[3,24,512]{2,1,0:T(8,128)(2,1)S(1)}, u32[]{:S(2)}, u32[]{:S(2)}) collective-permute-start(bf16[3,24,512]{2,1,0:T(8,128)(2,1)S(1)} %slice.75), channel_id=1, source_target_pairs={{0,480},{32,0},{64,32},{96,64},{128,96},{160,128},{192,160},{224,1... | collective-permute-start | bytes 221192 | tf_op jit(solution)/shard_map/ppermute | solution.py:17
  225.8 6.4 %collective-permute-start.5 = (bf16[21,6,512]{2,1,0:T(8,128)(2,1)S(1)}, bf16[21,6,512]{2,1,0:T(8,128)(2,1)S(1)}, u32[]{:S(2)}, u32[]{:S(2)}) collective-permute-start(bf16[21,6,512]{2,1,0:T(8,128)(2,1)S(1)} %pad_maximum_fusion.9), channel_id=1, source_target_pairs={{0,31},{1,0},{2,1},{3,2},{4,3},{5,4},{6,5},{7,6},{8,7},{9,8},{10,9... | collective-permute-start | bytes 387080 | tf_op jit(solution)/shard_map/ppermute | solution.py:17
  246.0 3.2 %fusion.35 = bf16[6,72,1,8,64]{1,4,3,0,2:T(8,128)(2,1)} fusion(bf16[6,72,8,64]{1,3,2,0:T(8,128)(2,1)} %bitcast.89, f32[6,8,72,72]{2,3,1,0:T(8,128)} %get-tuple-element.12, f32[6,8,72]{2,1,0:T(8,128)} %copy-done.7), kind=kOutput, calls=%fused_computation.38 | convolution fusion | flops 32569344 | bytes 1893888 | tf_op jit(solution)/shard_map/bhqk,bqhd->bkhd/dot_general | solution.py:21
  251.2 4.9 %fusion.32 = bf16[6,72,1,8,64]{1,4,3,0,2:T(8,128)(2,1)} fusion(f32[6,8,72,72]{2,3,1,0:T(8,128)} %fusion.63, bf16[6,72,1,8,64]{1,4,3,0,2:T(8,128)(2,1)} %copy.45, f32[6,8,72,72]{2,3,1,0:T(8,128)} %get-tuple-element.12, f32[6,8,72]{2,1,0:T(8,128)S(1)} %copy-done.8), kind=kOutput, calls=%fused_computation.37 | convolution fusion | flops 33817032 | bytes 2889216 | tf_op jit(solution)/shard_map/bhqk,bkhd->bqhd/dot_general | solution.py:21
  256.1 5.0 %fusion.29 = bf16[6,72,1,8,64]{1,4,3,0,2:T(8,128)(2,1)} fusion(f32[6,8,72,72]{2,3,1,0:T(8,128)} %fusion.63, bf16[6,72,1,8,64]{1,4,3,0,2:T(8,128)(2,1)} %copy-done.4, f32[6,8,72,72]{2,3,1,0:T(8,128)} %get-tuple-element.12, f32[6,8,72]{2,1,0:T(8,128)S(1)} %copy-done.8), kind=kOutput, calls=%fused_computation.36 | convolution fusion | flops 33817032 | bytes 2889216 | tf_op jit(solution)/shard_map/bhqk,bqhd->bkhd/dot_general | solution.py:21
  261.1 3.4 %pad_maximum_fusion = bf16[6,72,3,8,64]{1,4,3,0,2:T(8,128)(2,1)} fusion(bf16[6,72,1,8,64]{1,4,3,0,2:T(8,128)(2,1)S(1)} %copy-done.3, bf16[6,72,1,8,64]{1,4,3,0,2:T(8,128)(2,1)} %fusion.29, bf16[6,72,1,8,64]{1,4,3,0,2:T(8,128)(2,1)} %fusion.32), kind=kLoop, calls=%fused_computation.12 | loop fusion | flops 1327104 | bytes 2654208 | tf_op jit(solution)/shard_map/stack | solution.py:122
  264.5 5.5 %copy.35 = bf16[6,72,3,8,64]{4,3,2,1,0:T(8,128)(2,1)} copy(bf16[6,72,3,8,64]{1,4,3,0,2:T(8,128)(2,1)} %pad_maximum_fusion) | data formatting | bytes 2654208 | tf_op jit(solution)/shard_map/stack | solution.py:122
  270.0 4.5 %reshape.143 = bf16[6,72,1536]{2,1,0:T(8,128)(2,1)} reshape(bf16[6,72,3,8,64]{4,3,2,1,0:T(8,128)(2,1)} %copy.35) | data formatting | bytes 2654208 | tf_op jit(solution)/shard_map/reshape | solution.py:123
  281.3 7.7 %collective-permute-done.6 = bf16[18,6,512]{2,1,0:T(8,128)(2,1)S(1)} collective-permute-done((bf16[18,6,512]{2,1,0:T(8,128)(2,1)S(1)}, bf16[18,6,512]{2,1,0:T(8,128)(2,1)S(1)}, u32[]{:S(2)}, u32[]{:S(2)}) %collective-permute-start.6) | collective-permute-done | bytes 110624 | tf_op jit(solution)/shard_map/ppermute | solution.py:17
  290.9 4.5 %fusion.37 = bf16[432,512]{1,0:T(8,128)(2,1)} fusion(f32[432,512]{1,0:T(8,128)S(1)} %bitcast.86, bf16[2048,512]{1,0:T(8,128)(2,1)} %all-gather.8.cloned.1.call-done, f32[432,2048]{1,0:T(8,128)} %fusion.68), kind=kOutput, calls=%fused_computation.40 | convolution fusion | flops 910835712 | bytes 6963200 | tf_op jit(solution)/shard_map/nf,fc->nc/dot_general | solution.py:21
  (87 shorter events, 57.2 us)
Async XLA Ops:
  7.2 10.0 %copy-start.6 = (bf16[32,512]{1,0:T(8,128)(2,1)S(1)}, bf16[32,512]{1,0:T(8,128)(2,1)}, u32[]{:S(2)}) copy-start(bf16[32,512]{1,0:T(8,128)(2,1)} %param.9) | copy-start | bytes 98308
  7.2 69.0 %all-gather.4.cloned.1.call-start = ((), (), s32[]{:S(2)}) async-start(), calls=%async_computation | async-start | bytes 1671168 | tf_op jit(solution)/shard_map/all_gather | solution.py:131
  7.9 134.3 %all-gather.6.cloned.1.call-start = ((), (), s32[]{:S(2)}) async-start(), calls=%async_computation.1 | async-start | bytes 2228224 | tf_op jit(solution)/shard_map/all_gather | solution.py:133
  8.7 199.6 %all-gather.8.cloned.1.call-start = ((), (), s32[]{:S(2)}) async-start(), calls=%async_computation.2 | async-start | bytes 2228224 | tf_op jit(solution)/shard_map/all_gather | solution.py:134
  12.4 26.2 %collective-permute-start = (bf16[3,24,512]{2,1,0:T(8,128)(2,1)S(1)}, bf16[3,24,512]{2,1,0:T(8,128)(2,1)S(1)}, u32[]{:S(2)}, u32[]{:S(2)}) collective-permute-start(bf16[3,24,512]{2,1,0:T(8,128)(2,1)S(1)} %slice.70), channel_id=1, source_target_pairs={{0,480},{32,0},{64,32},{96,64},{128,96},{160,128},{192,160},{224,1... | collective-permute-start | bytes 221192 | tf_op jit(solution)/shard_map/ppermute | solution.py:17
  38.6 15.0 %collective-permute-start.1 = (bf16[21,6,512]{2,1,0:T(8,128)(2,1)S(1)}, bf16[21,6,512]{2,1,0:T(8,128)(2,1)S(1)}, u32[]{:S(2)}, u32[]{:S(2)}) collective-permute-start(bf16[21,6,512]{2,1,0:T(8,128)(2,1)S(1)} %pad_maximum_fusion.10), channel_id=1, source_target_pairs={{0,31},{1,0},{2,1},{3,2},{4,3},{5,4},{6,5},{7,6},{8,7},{9,8},{10,9... | collective-permute-start | bytes 387080 | tf_op jit(solution)/shard_map/ppermute | solution.py:17
  84.6 3.6 %copy-start.1 = (bf16[6,72,1,8,64]{4,3,2,1,0:T(8,128)(2,1)S(1)}, bf16[6,72,1,8,64]{4,3,2,1,0:T(8,128)(2,1)}, u32[]{:S(2)}) copy-start(bf16[6,72,1,8,64]{4,3,2,1,0:T(8,128)(2,1)} %get-tuple-element.10) | copy-start | bytes 1327108
  86.3 6.6 %copy-start.4 = (bf16[6,72,1,8,64]{1,4,3,0,2:T(8,128)(2,1)}, bf16[6,72,1,8,64]{1,4,3,0,2:T(8,128)(2,1)S(1)}, u32[]{:S(2)}) copy-start(bf16[6,72,1,8,64]{1,4,3,0,2:T(8,128)(2,1)S(1)} %copy.44) | copy-start | bytes 1327108
  86.3 3.3 %copy-start.5 = (pred[6,72,72]{1,2,0:T(8,128)(4,1)S(1)}, pred[6,72,72]{1,2,0:T(8,128)(4,1)}, u32[]{:S(2)}) copy-start(pred[6,72,72]{1,2,0:T(8,128)(4,1)} %broadcast_compare_fusion) | copy-start | bytes 93316
  92.9 1.9 copy-start.7
  95.4 21.5 %copy-start = (bf16[18,24,512]{2,1,0:T(8,128)(2,1)S(1)}, bf16[18,24,512]{2,1,0:T(8,128)(2,1)}, u32[]{:S(2)}) copy-start(bf16[18,24,512]{2,1,0:T(8,128)(2,1)} %param.6) | copy-start | bytes 1327108
  97.5 10.0 %collective-permute-start.2 = (bf16[18,6,512]{2,1,0:T(8,128)(2,1)S(1)}, bf16[18,6,512]{2,1,0:T(8,128)(2,1)S(1)}, u32[]{:S(2)}, u32[]{:S(2)}) collective-permute-start(bf16[18,6,512]{2,1,0:T(8,128)(2,1)S(1)} %slice.74), channel_id=1, source_target_pairs={{0,1},{1,2},{2,3},{3,4},{4,5},{5,6},{6,7},{7,8},{8,9},{9,10},{10,1... | collective-permute-start | bytes 331784 | tf_op jit(solution)/shard_map/ppermute | solution.py:17
  107.5 9.3 %collective-permute-start.3 = (bf16[3,24,512]{2,1,0:T(8,128)(2,1)S(1)}, bf16[3,24,512]{2,1,0:T(8,128)(2,1)S(1)}, u32[]{:S(2)}, u32[]{:S(2)}) collective-permute-start(bf16[3,24,512]{2,1,0:T(8,128)(2,1)S(1)} %pad_maximum_fusion.12), channel_id=1, source_target_pairs={{0,32},{32,64},{64,96},{96,128},{128,160},{160,192},{192,224},{224... | collective-permute-start | bytes 221192 | tf_op jit(solution)/shard_map/ppermute | solution.py:17
  218.1 7.7 %collective-permute-start.4 = (bf16[3,24,512]{2,1,0:T(8,128)(2,1)S(1)}, bf16[3,24,512]{2,1,0:T(8,128)(2,1)S(1)}, u32[]{:S(2)}, u32[]{:S(2)}) collective-permute-start(bf16[3,24,512]{2,1,0:T(8,128)(2,1)S(1)} %slice.75), channel_id=1, source_target_pairs={{0,480},{32,0},{64,32},{96,64},{128,96},{160,128},{192,160},{224,1... | collective-permute-start | bytes 221192 | tf_op jit(solution)/shard_map/ppermute | solution.py:17
  225.8 9.1 %collective-permute-start.5 = (bf16[21,6,512]{2,1,0:T(8,128)(2,1)S(1)}, bf16[21,6,512]{2,1,0:T(8,128)(2,1)S(1)}, u32[]{:S(2)}, u32[]{:S(2)}) collective-permute-start(bf16[21,6,512]{2,1,0:T(8,128)(2,1)S(1)} %pad_maximum_fusion.9), channel_id=1, source_target_pairs={{0,31},{1,0},{2,1},{3,2},{4,3},{5,4},{6,5},{7,6},{8,7},{9,8},{10,9... | collective-permute-start | bytes 387080 | tf_op jit(solution)/shard_map/ppermute | solution.py:17
  246.0 3.2 %copy-start.2 = (bf16[6,72,512]{1,2,0:T(8,128)(2,1)S(1)}, bf16[6,72,512]{1,2,0:T(8,128)(2,1)}, u32[]{:S(2)}) copy-start(bf16[6,72,512]{1,2,0:T(8,128)(2,1)} %copy.42) | copy-start | bytes 1327108
  249.3 1.9 copy-start.8
  256.1 5.0 %copy-start.3 = (bf16[6,72,1,8,64]{1,4,3,0,2:T(8,128)(2,1)S(1)}, bf16[6,72,1,8,64]{1,4,3,0,2:T(8,128)(2,1)}, u32[]{:S(2)}) copy-start(bf16[6,72,1,8,64]{1,4,3,0,2:T(8,128)(2,1)} %fusion.35) | copy-start | bytes 1327108
  279.3 9.6 %collective-permute-start.6 = (bf16[18,6,512]{2,1,0:T(8,128)(2,1)S(1)}, bf16[18,6,512]{2,1,0:T(8,128)(2,1)S(1)}, u32[]{:S(2)}, u32[]{:S(2)}) collective-permute-start(bf16[18,6,512]{2,1,0:T(8,128)(2,1)S(1)} %slice.76), channel_id=1, source_target_pairs={{0,1},{1,2},{2,3},{3,4},{4,5},{5,6},{6,7},{7,8},{8,9},{9,10},{10,1... | collective-permute-start | bytes 331784 | tf_op jit(solution)/shard_map/ppermute | solution.py:17
  289.0 9.3 %collective-permute-start.7 = (bf16[3,24,512]{2,1,0:T(8,128)(2,1)S(1)}, bf16[3,24,512]{2,1,0:T(8,128)(2,1)S(1)}, u32[]{:S(2)}, u32[]{:S(2)}) collective-permute-start(bf16[3,24,512]{2,1,0:T(8,128)(2,1)S(1)} %pad_maximum_fusion.11), channel_id=1, source_target_pairs={{0,32},{32,64},{64,96},{96,128},{128,160},{160,192},{192,224},{224... | collective-permute-start | bytes 221192 | tf_op jit(solution)/shard_map/ppermute | solution.py:17
Sparse Core Ops, SparseCore 0:
  11.3 64.7 all-gather.3
  79.5 62.6 all-gather.5
  145.5 62.7 all-gather.7
where the time goes:
time: 309 us; the launch traced here: 307 us
  waiting for transfers between devices  142 us (46%)
  matrix products  45.3 us (15%)
  starting transfers between devices  37.1 us (12%)
  local copies, waits for them, and re-layouts  32.9 us (11%)
  blocking collectives  21.2 us (7%)
  between operations  14.1 us (5%)
  other arithmetic  13.7 us (4%)
    all_gather x1, waiting for transfers between devices, shards(): lax.all_gather(contract_weight, 'lat', axis=0, tiled=True)  61.6 us
    dot_general x12, matrix products, product(): jnp.einsum(pattern, operand, other, preferred_element_type=jnp.float32)  42 us
    ppermute x8, starting transfers between devices, shifted_2(): return lax.ppermute(value, axis, pairs)  37 us
    ppermute x8, waiting for transfers between devices, shifted_2(): return lax.ppermute(value, axis, pairs)  32.5 us
    all_gather x1, waiting for transfers between devices, shards(): lax.all_gather(expand_weight, 'lat', axis=0, tiled=True)  24.4 us
    all_gather x1, waiting for transfers between devices, shards(): lax.all_gather(qkv_weight, 'lat', axis=0, tiled=True)  22.1 us
    all_gather x1, blocking collectives, shards(): lax.all_gather(proj_weight, 'lat', axis=0, tiled=True)  21.2 us
  transfers between devices with their start and end apart: 11, of which 10 were waited for; matrix products, arithmetic and copies ran while one was open for 12% of the time, Pallas kernels for 0%

commit v1 on v0

v1 whole, which is shorter than its diff:
```python
import jax
import jax.numpy as jnp
from jax import lax
from jax.experimental import pallas as pl
from jax.experimental.pallas import tpu as pltpu
from jax.sharding import PartitionSpec as P

HEADS = 8
WIN_LAT = 6
WIN_LON = 12
ROWS = 18
COLS = 24
WIN = WIN_LAT * WIN_LON
NW = 6
T = ROWS * COLS
C = 512
FF = 2048
EPSILON = 1e-05
F32 = jnp.float32
BF16 = jnp.bfloat16
MESH = pl.DeviceIdType.MESH

RIM_EAST, RIM_SOUTH, RIM_CORNER, RIM_END = 0, 96, 160, 192

SHAPES = ((32, 1536), (32, 512), (32, 2048), (128, 512))

A1, A2, B1P, B1M, B2P, B2M, B3P, B3M, CP, CM, CS = range(11)
D_OWN, D_CROSS, D_XM, D_XP, D_X2, D_ZP, D_ZM, D_Z2 = range(11, 19)
MESSAGES = 19


def nn(a, b):
    return lax.dot_general(a, b, (((1,), (0,)), ((), ())), preferred_element_type=F32)


def nt(a, b):
    return lax.dot_general(a, b, (((1,), (1,)), ((), ())), preferred_element_type=F32)


def tn(a, b):
    return lax.dot_general(a, b, (((0,), (0,)), ((), ())), preferred_element_type=F32)


def normalize(values):
    average = jnp.mean(values, axis=-1, keepdims=True)
    centred = values - average
    inverse = lax.rsqrt(jnp.mean(centred * centred, axis=-1, keepdims=True) + EPSILON)
    return centred * inverse, inverse


def normalize_back(scaled, inverse, gradient):
    mean_grad = jnp.mean(gradient, axis=-1, keepdims=True)
    projected = jnp.mean(gradient * scaled, axis=-1, keepdims=True)
    return inverse * (gradient - mean_grad - scaled * projected)


def gelu_parts(u):
    phi = 0.5 + 0.5 * lax.erf(u * 0.7071067811865476)
    return phi, u * jnp.exp(-0.5 * u * u) * 0.3989422804014327


def head_rows(part):
    lane = lax.broadcasted_iota(jnp.int32, (WIN, 256), 1)
    return jnp.concatenate(
        [jnp.where((lane >= 64 * h) & (lane < 64 * (h + 1)), part, 0.0) for h in range(4)], axis=0
    ).astype(BF16)


def head_lanes(rows):
    lane = lax.broadcasted_iota(jnp.int32, (WIN, 256), 1)
    out = rows[:WIN]
    for h in range(1, 4):
        out = jnp.where(lane >= 64 * h, rows[WIN * h : WIN * (h + 1)], out)
    return out


def segments():
    runs = []
    for j in range(ROWS):
        base = (j // WIN_LAT) * 2 * WIN + (j % WIN_LAT) * WIN_LON
        if j < ROWS - 3:
            runs.append((base, 12, j + 3, 6, None))
            runs.append((base + WIN, 6, j + 3, 18, None))
            runs.append((base + WIN + 6, 6, None, None, RIM_EAST + 6 * j))
        else:
            south = RIM_SOUTH + 18 * (j - 15)
            runs.append((base, 12, None, None, south))
            runs.append((base + WIN, 6, None, None, south + 12))
            runs.append((base + WIN + 6, 6, None, None, RIM_CORNER + 6 * (j - 15)))
    return runs


def pack_rim(tile, rim32, rim):
    for j in range(15):
        rim32[RIM_EAST + 6 * j : RIM_EAST + 6 * j + 6] = tile[j + 3].astype(F32)[:6]
    for j in range(3):
        row = tile[j].astype(F32)
        rim32[RIM_SOUTH + 18 * j : RIM_SOUTH + 18 * j + 18] = row[6:]
        rim32[RIM_CORNER + 6 * j : RIM_CORNER + 6 * j + 6] = row[:6]
    rim[...] = rim32[...].astype(BF16)


def to_windows(tile, rim32, out):
    for start, count, row, col, other in segments():
        if other is None:
            out[start : start + count] = tile[row].astype(F32)[col : col + count]
        else:
            out[start : start + count] = rim32[other : other + count]


def from_windows(values, tile32, rim32):
    for start, count, row, col, other in segments():
        if other is None:
            tile32[row, col : col + count] = values[start : start + count]
        else:
            rim32[other : other + count] = values[start : start + count]


def place_rim(rim32, tile32):
    for j in range(15):
        tile32[j + 3, :6] = rim32[RIM_EAST + 6 * j : RIM_EAST + 6 * j + 6]
    for j in range(3):
        tile32[j, 6:] = rim32[RIM_SOUTH + 18 * j : RIM_SOUTH + 18 * j + 18]
        tile32[j, :6] = rim32[RIM_CORNER + 6 * j : RIM_CORNER + 6 * j + 6]


def make_bias(flag):
    row = lax.rem(lax.broadcasted_iota(jnp.int32, (4 * WIN, 128), 0), WIN)
    key = lax.broadcasted_iota(jnp.int32, (4 * WIN, 128), 1)
    plain = jnp.where(key < WIN, 0.0, -1e30)
    cut = jnp.where((row >= WIN // 2) != (key >= WIN // 2), -1e30, plain)
    return plain, jnp.where(flag, cut, plain)


def flat(ref):
    return ref[...].astype(F32).reshape(T, C).astype(BF16)


def kernel(
    tok_h, gra_h, wq_h, wp_h, we_h, wc_h, out_ref, gt_ref,
    tok, gra, wq, wp, we, wc, send_sem, recv_sem, load_sem, rim_send_sem, rim_recv_sem,
    rim32, rim_out, rim_in, x_ref, gw_ref, sc_ref, q_ref, k_ref, v_ref, p_ref, m_ref, bias_ref,
    oacc, gacc, gh_ref, gq_ref, gk_ref, gv_ref, o_tile, g_tile,
):
    lat, lon = lax.axis_index("lat"), lax.axis_index("lon")
    hi, x, c = lat // 8, lax.rem(lat // 2, 4), lax.rem(lat, 2)
    lo, z = lon // 16, lax.rem(lon, 16)
    colour = lax.rem(lo + z, 2)
    other = 1 - colour
    xp, xm, x2 = lax.rem(x + 1, 4), lax.rem(x + 3, 4), lax.rem(x + 2, 4)

    def at(hi_, x_, c_, lo_, z_):
        return (hi_ * 8 + x_ * 2 + c_, lo_ * 16 + z_)

    core = at(hi, x, 1 - c, lo, z)
    to_xp, to_xm = at(hi, xp, c, lo, z), at(hi, xm, c, lo, z)
    same, cross = at(hi, x, c, 1 - lo, z), at(1 - hi, x, c, 1 - lo, z)
    to_zp, to_zm = at(hi, x, c, lo, lax.rem(z + 1, 16)), at(hi, x, c, lo, lax.rem(z + 15, 16))
    north, south = lax.rem(lat + 15, 16), lax.rem(lat + 1, 16)
    west, east = lax.rem(lon + 31, 32), lax.rem(lon + 1, 32)
    back = ((lat, west), (north, lon), (north, west))
    ahead = ((lat, east), (south, lon), (south, east))

    weights = (wq, wp, we, wc)
    loads = [
        pltpu.make_async_copy(source, target, load_sem.at[n])
        for n, (source, target) in enumerate(
            [(h, w.at[hi, x, c]) for h, w in zip((wq_h, wp_h, we_h, wc_h), weights)]
            + [(tok_h, tok), (gra_h, gra)]
        )
    ]
    for load in loads:
        load.start()

    barrier = pltpu.get_barrier_semaphore()
    friends = (core, to_xp, to_xm, same, cross, to_zp, to_zm) + back + ahead
    for friend in friends:
        pl.semaphore_signal(barrier, inc=1, device_id=friend, device_id_type=MESH)
    k_ref[:, WIN:, :] = jnp.zeros((NW, 128 - WIN, C), BF16)
    v_ref[:, WIN:, :] = jnp.zeros((NW, 128 - WIN, C), BF16)
    plain, cut = make_bias(lat == lax.axis_size("lat") - 1)
    bias_ref[0] = plain
    bias_ref[1] = cut
    for load in loads:
        load.wait()
    rim32[...] = jnp.zeros((RIM_END, C), F32)
    pl.semaphore_wait(barrier, len(friends))

    started = []

    def message(i, number, slab, target):
        ref = weights[i].at[slab]
        return pltpu.make_async_remote_copy(
            src_ref=ref, dst_ref=ref, send_sem=send_sem.at[i, number], recv_sem=recv_sem.at[i, number],
            device_id=target, device_id_type=MESH,
        )

    def send(i, number, slab, target):
        copy = message(i, number, slab, target)
        copy.start()
        started.append(copy)

    def arrived(i, number, slab):
        message(i, number, slab, core).wait_recv()

    every = slice(None)

    def stage0(i):
        send(i, A1, (hi, x, c, other), cross)
        send(i, B1P, (hi, x, c, colour), to_xp)
        send(i, B1M, (hi, x, c, colour), to_xm)
        send(i, A2, (hi, x, c, colour), cross)
        send(i, D_OWN, (hi, x, c), core)

    def stage1(i):
        arrived(i, A1, (1 - hi, x, c, colour))
        send(i, B2P, (1 - hi, x, c, colour), to_xp)
        send(i, B2M, (1 - hi, x, c, colour), to_xm)

    def stage2(i):
        half = SHAPES[i][1] // 2
        arrived(i, B1P, (hi, xm, c, colour))
        arrived(i, B2P, (1 - hi, xm, c, colour))
        send(i, B3P, (every, xm, c, colour, every, slice(0, half)), to_xp)
        arrived(i, B1M, (hi, xp, c, colour))
        arrived(i, B2M, (1 - hi, xp, c, colour))
        send(i, B3M, (every, xp, c, colour, every, slice(half, 2 * half)), to_xm)
        send(i, CM, (every, xm, c, colour), to_zm)
        send(i, CP, (every, xp, c, colour), to_zp)
        send(i, D_XM, (every, xm, c, colour), core)
        send(i, D_XP, (every, xp, c, colour), core)

    def stage3(i):
        half = SHAPES[i][1] // 2
        arrived(i, B3P, (every, x2, c, colour, every, slice(0, half)))
        arrived(i, B3M, (every, x2, c, colour, every, slice(half, 2 * half)))
        send(i, CS, (every, x2, c, colour), same)
        send(i, D_X2, (every, x2, c, colour), core)
        arrived(i, A2, (1 - hi, x, c, other))
        send(i, D_CROSS, (1 - hi, x, c), core)

    def stage4(i):
        arrived(i, CP, (every, xp, c, other))
        send(i, D_ZP, (every, xp, c, other), core)
        arrived(i, CM, (every, xm, c, other))
        send(i, D_ZM, (every, xm, c, other), core)
        arrived(i, CS, (every, x2, c, other))
        send(i, D_Z2, (every, x2, c, other), core)

    def stage5(i):
        d = 1 - c
        arrived(i, D_OWN, (hi, x, d))
        arrived(i, D_CROSS, (1 - hi, x, d))
        arrived(i, D_XM, (every, xm, d, colour))
        arrived(i, D_XP, (every, xp, d, colour))
        arrived(i, D_X2, (every, x2, d, colour))
        arrived(i, D_ZP, (every, xp, d, other))
        arrived(i, D_ZM, (every, xm, d, other))
        arrived(i, D_Z2, (every, x2, d, other))

    bounds = ((RIM_EAST, RIM_SOUTH), (RIM_SOUTH, RIM_CORNER), (RIM_CORNER, RIM_END))

    def rims(slot, targets):
        return [
            pltpu.make_async_remote_copy(
                src_ref=rim_out.at[slot, pl.ds(a, b - a)], dst_ref=rim_in.at[slot, pl.ds(a, b - a)],
                send_sem=rim_send_sem.at[slot, n], recv_sem=rim_recv_sem.at[slot, n],
                device_id=target, device_id_type=MESH,
            )
            for n, ((a, b), target) in enumerate(zip(bounds, targets))
        ]

    def send_rims(slot, targets):
        for copy in rims(slot, targets):
            copy.start()
            started.append(copy)

    def take_rims(slot, targets):
        for copy in rims(slot, targets):
            copy.wait_recv()
        rim32[...] = rim_in[slot].astype(F32)

    stage0(0)
    pack_rim(tok, rim32, rim_out.at[0])
    send_rims(0, back)
    stage0(1)
    stage1(0)
    stage1(1)
    stage0(2)
    stage2(0)
    pack_rim(gra, rim32, rim_out.at[1])
    send_rims(1, back)
    stage1(2)
    stage0(3)
    stage3(0)
    stage2(1)
    take_rims(0, back)
    to_windows(tok, rim32, x_ref)
    values = x_ref[...]
    scaled1, inverse1 = normalize(values)
    sc_ref[...] = scaled1
    normal1 = scaled1.astype(BF16)
    stage4(0)
    stage3(1)
    stage1(3)
    stage5(0)

    def whole(i, cols):
        rows = SHAPES[i][0] * 16
        return weights[i][:, :, :, :, :, cols].reshape(rows, cols.stop - cols.start)

    for n, ref in enumerate((q_ref, k_ref, v_ref)):
        part = nn(normal1, whole(0, slice(C * n, C * (n + 1))))
        if n == 0:
            part = part.astype(BF16).astype(F32) * 0.125
        ref[:, :WIN, :] = part.reshape(NW, WIN, C).astype(BF16)

    def attend(w, quad):
        lanes = slice(256 * quad, 256 * (quad + 1))
        queries = head_rows(q_ref[w, :, lanes].astype(F32))
        scores = nt(queries, k_ref[w, :, lanes]) + bias_ref[w // 4]
        exponent = jnp.exp(scores - jnp.max(scores, axis=-1, keepdims=True))
        probs = exponent * (1.0 / jnp.sum(exponent, axis=-1, keepdims=True))
        p_ref[2 * w + quad] = probs
        m_ref[w, :, lanes] = head_lanes(nn(probs.astype(BF16), v_ref[w, :, lanes])).astype(BF16)

    service = {1: (stage2, 2), 3: (stage4, 1), 5: (stage3, 2), 7: (stage2, 3), 9: (stage4, 2), 10: (stage3, 3)}
    for n in range(12):
        attend(n // 2, n % 2)
        if n in service:
            stage, i = service[n]
            stage(i)

    stage5(1)
    attn = nn(flat(m_ref), whole(1, slice(0, C))).astype(BF16).astype(F32)
    hidden = x_ref[...] + attn
    scaled2, inverse2 = normalize(hidden)
    normal2 = scaled2.astype(BF16)
    take_rims(1, back)
    to_windows(gra, rim32, gw_ref)
    gradient = gw_ref[...].astype(BF16)
    stage4(3)
    stage5(2)
    stage5(3)

    chunk = 512
    for f in range(FF // chunk):
        expand = whole(2, slice(chunk * f, chunk * (f + 1)))
        contract = wc[f // 2, 2 * (f % 2) : 2 * (f % 2) + 2].reshape(chunk, C)
        preact = nn(normal2, expand)
        grad_act = nt(gradient, contract)
        phi, tail = gelu_parts(preact)
        feed = nn((preact * phi).astype(BF16), contract)
        grad_norm2 = nt((grad_act * (phi + tail)).astype(BF16), expand)
        if f == 0:
            oacc[...] = feed
            gacc[...] = grad_norm2
        else:
            oacc[...] += feed
            gacc[...] += grad_norm2

    from_windows(hidden + oacc[...], o_tile, rim32)
    rim_out[2] = rim32[...].astype(BF16)
    send_rims(2, ahead)

    grad_hidden = gw_ref[...] + normalize_back(scaled2, inverse2, gacc[...])
    gh_ref[...] = grad_hidden
    proj = whole(1, slice(0, C))
    m_ref[...] = nt(grad_hidden.astype(BF16), proj).reshape(NW, WIN, C).astype(BF16)

    def attend_back(w, quad):
        lanes = slice(256 * quad, 256 * (quad + 1))
        grad_mixed = head_rows(m_ref[w, :, lanes].astype(F32))
        queries = head_rows(q_ref[w, :, lanes].astype(F32))
        probs = p_ref[2 * w + quad]
        grad_probs = nt(grad_mixed, v_ref[w, :, lanes])
        grad_scores = probs * (grad_probs - jnp.sum(grad_probs * probs, axis=-1, keepdims=True))
        grad_scores = grad_scores.astype(BF16)
        grad_queries = head_lanes(nn(grad_scores, k_ref[w, :, lanes])) * 0.125
        gq_ref[w, :, lanes] = grad_queries.astype(BF16)
        gk_ref[w, :, lanes] = tn(grad_scores, queries)[:WIN].astype(BF16)
        gv_ref[w, :, lanes] = tn(probs.astype(BF16), grad_mixed)[:WIN].astype(BF16)

    for n in range(12):
        attend_back(n // 2, n % 2)

    grad_normal1 = (
        nt(flat(gq_ref), whole(0, slice(0, C)))
        + nt(flat(gk_ref), whole(0, slice(C, 2 * C)))
        + nt(flat(gv_ref), whole(0, slice(2 * C, 3 * C)))
    )
    grad_normal1 = grad_normal1.astype(BF16).astype(F32)
    x_ref[...] = gh_ref[...] + normalize_back(sc_ref[...], inverse1, grad_normal1)
    from_windows(x_ref, g_tile, rim32)
    rim_out[3] = rim32[...].astype(BF16)
    send_rims(3, ahead)

    take_rims(2, ahead)
    place_rim(rim32, o_tile)
    out_ref[...] = o_tile[...].astype(BF16)
    take_rims(3, ahead)
    place_rim(rim32, g_tile)
    gt_ref[...] = g_tile[...].astype(BF16)
    for copy in started:
        copy.wait_send()


def shards(tokens, grad_output, qkv_weight, proj_weight, expand_weight, contract_weight):
    packed = [
        weight.reshape(2, rows // 2, columns)
        for weight, (rows, columns) in zip(
            (qkv_weight, proj_weight, expand_weight, contract_weight), SHAPES
        )
    ]
    anywhere = pl.BlockSpec(memory_space=pl.ANY)
    vmem = pl.BlockSpec(memory_space=pltpu.VMEM)
    return pl.pallas_call(
        kernel,
        out_shape=[jax.ShapeDtypeStruct((ROWS, COLS, C), BF16)] * 2,
        in_specs=[anywhere] * 6,
        out_specs=[vmem] * 2,
        scratch_shapes=[
            pltpu.VMEM((ROWS, COLS, C), BF16),
            pltpu.VMEM((ROWS, COLS, C), BF16),
        ]
        + [pltpu.VMEM((2, 4, 2, 2, rows // 2, columns), BF16) for rows, columns in SHAPES]
        + [
            pltpu.SemaphoreType.DMA((4, MESSAGES)),
            pltpu.SemaphoreType.DMA((4, MESSAGES)),
            pltpu.SemaphoreType.DMA((6,)),
            pltpu.SemaphoreType.DMA((4, 3)),
            pltpu.SemaphoreType.DMA((4, 3)),
            pltpu.VMEM((RIM_END, C), F32),
            pltpu.VMEM((4, RIM_END, C), BF16),
            pltpu.VMEM((4, RIM_END, C), BF16),
            pltpu.VMEM((T, C), F32),
            pltpu.VMEM((T, C), F32),
            pltpu.VMEM((T, C), F32),
            pltpu.VMEM((NW, WIN, C), BF16),
            pltpu.VMEM((NW, 128, C), BF16),
            pltpu.VMEM((NW, 128, C), BF16),
            pltpu.VMEM((12, 4 * WIN, 128), F32),
            pltpu.VMEM((NW, WIN, C), BF16),
            pltpu.VMEM((2, 4 * WIN, 128), F32),
            pltpu.VMEM((T, C), F32),
            pltpu.VMEM((T, C), F32),
            pltpu.VMEM((T, C), F32),
            pltpu.VMEM((NW, WIN, C), BF16),
            pltpu.VMEM((NW, WIN, C), BF16),
            pltpu.VMEM((NW, WIN, C), BF16),
            pltpu.VMEM((ROWS, COLS, C), F32),
            pltpu.VMEM((ROWS, COLS, C), F32),
        ],
        compiler_params=pltpu.CompilerParams(
            collective_id=0, has_side_effects=True, vmem_limit_bytes=56 * 2**20
        ),
        name="swin_block",
    )(tokens, grad_output, *packed)


def solution(mesh):
    return jax.shard_map(
        shards,
        mesh=mesh,
        in_specs=(
            P("lat", "lon", None),
            P("lat", "lon", None),
            P("lat", None),
            P("lat", None),
            P("lat", None),
            P("lat", None),
        ),
        out_specs=(P("lat", "lon", None), P("lat", "lon", None)),
        check_vma=False,
    )
```

time: 309 us -> 69.4 us (0.22)
  waiting for transfers between devices: 142 us -> 0 us
  Pallas kernels: 0 us -> 65 us
  matrix products: 45.3 us -> 0 us
  starting transfers between devices: 37.1 us -> 0 us
  local copies, waits for them, and re-layouts: 32.9 us -> 2.62 us
  blocking collectives: 21.2 us -> 0 us
  other arithmetic: 13.7 us -> 0 us
  between operations: 14.1 us -> 0.65 us
    all_gather x3 -> x0, waiting for transfers between devices: 108 us -> none  [the longest x1 61.6 us: shards(): lax.all_gather(contract_weight, 'lat', axis=0, tiled=True)]
    pallas_call x0 -> x1, Pallas kernels: none -> 65 us  [shards(): pl.pallas_call(kernel, out_shape=[jax.ShapeDtypeStruct((ROWS, COLS, C), B...]
    dot_general x12 -> x0, matrix products: 42 us -> none  [product(): jnp.einsum(pattern, operand, other, preferred_element_type=jnp.float32)]
    ppermute x8 -> x0, starting transfers between devices: 37 us -> none  [shifted_2(): return lax.ppermute(value, axis, pairs)]
    ppermute x8 -> x0, waiting for transfers between devices: 32.5 us -> none  [shifted_2(): return lax.ppermute(value, axis, pairs)]
    all_gather x1 -> x0, blocking collectives: 21.2 us -> none  [shards(): lax.all_gather(proj_weight, 'lat', axis=0, tiled=True)]
    reshape x11 -> x0, local copies, waits for them, and re-layouts: 16.5 us -> none  [the longest x1 4.48 us: attend_back(): grad_proj.reshape(window_count, length, 3 * heads_here * head_size)]
    another operation x1 -> x0, local copies, waits for them, and re-layouts: 5.49 us -> none  [attend_back(): grad_proj = jnp.stack([grad_queries, grad_keys, grad_values], axis=2)]
  transfers between devices with their start and end apart: 11 -> 0, of which waited for: 10 -> 0; matrix products, arithmetic and copies ran while one was open for 12% -> 0% of each run, Pallas kernels for 0% -> 0%
where the time goes in v1:
time: 69.4 us; the launch traced here: 68.3 us
  Pallas kernels  65 us (94%)
  local copies, waits for them, and re-layouts  2.62 us (4%)
    pallas_call x1, Pallas kernels, shards(): pl.pallas_call(kernel, out_shape=[jax.ShapeDtypeStruct((ROWS, COLS, C), B...  65 us
    unnamed x4, local copies, waits for them, and re-layouts  2.62 us

profile of v1, /device:TPU:24, one launch (start us, length us, event | category | flops | bytes accessed | tf_op | source)
XLA Modules:
  0.0 68.3 jit_solution(6823178770965453954)
XLA Ops:
  0.6 65.0 %swin_block.1 = (bf16[18,24,512]{2,1,0:T(8,128)(2,1)}, bf16[18,24,512]{2,1,0:T(8,128)(2,1)}) custom-call(bf16[18,24,512]{2,1,0:T(8,128)(2,1)} %tok_h.1, bf16[18,24,512]{2,1,0:T(8,128)(2,1)} %gra_h.1, bf16[2,16,1536]{2,1,0:T(8,128)(2,1)} %bitcast.6, bf16[2,16,512]{2,1,0:T(8,128)(2,1)} %bitcast.7, bf16[2,16,2048]{2,1,0:T(8,128)(2,1)} %bitcast.4, ...), custom_call_target="tpu_custom_call" | custom-call | tf_op jit(solution)/shard_map/swin_block/pallas_call | solution.py:417
  65.6 0.0 copy-start
  65.7 1.9 %copy.10 = bf16[18,24,512]{2,1,0:T(8,128)(2,1)} copy(bf16[18,24,512]{2,1,0:T(8,128)(2,1)} %get-tuple-element.4) | data formatting | bytes 884736
  67.5 0.0 copy-done
  67.5 0.8 %copy.11 = bf16[18,24,512]{2,1,0:T(8,128)(2,1)} copy(bf16[18,24,512]{2,1,0:T(8,128)(2,1)S(1)} %copy-done) | data formatting | bytes 884736
Async XLA Ops:
  65.6 1.9 %copy-start = (bf16[18,24,512]{2,1,0:T(8,128)(2,1)S(1)}, bf16[18,24,512]{2,1,0:T(8,128)(2,1)}, u32[]{:S(2)}) copy-start(bf16[18,24,512]{2,1,0:T(8,128)(2,1)} %get-tuple-element.5) | copy-start | bytes 1327108

commit v2 on v1

--- a/solution.py
+++ b/solution.py
@@ -24,9 +24,17 @@
 
 SHAPES = ((32, 1536), (32, 512), (32, 2048), (128, 512))
 
-A1, A2, B1P, B1M, B2P, B2M, B3P, B3M, CP, CM, CS = range(11)
-D_OWN, D_CROSS, D_XM, D_XP, D_X2, D_ZP, D_ZM, D_Z2 = range(11, 19)
-MESSAGES = 19
+PIECES = (
+    (0, slice(0, 16), slice(0, 1536)),
+    (1, slice(0, 16), slice(0, 512)),
+    (2, slice(0, 16), slice(0, 2048)),
+    (3, slice(0, 32), slice(0, 512)),
+    (3, slice(32, 64), slice(0, 512)),
+)
+
+A1, A2, B1P, B1M, B2P, B2M, B3P, B3M, CP, CM, CS, CX = range(12)
+D_OWN, D_CROSS, D_XM, D_XP, D_X2, D_ZP, D_ZM, D_Z2 = range(12, 20)
+MESSAGES = 20
 
 
 def nn(a, b):
@@ -108,8 +116,10 @@
             out[start : start + count] = rim32[other : other + count]
 
 
-def from_windows(values, tile32, rim32):
+def from_windows(values, tile32, rim32, edge=None):
     for start, count, row, col, other in segments():
+        if edge is not None and edge == (start // WIN in (0, 2)):
+            continue
         if other is None:
             tile32[row, col : col + count] = values[start : start + count]
         else:
@@ -155,6 +165,7 @@
     core = at(hi, x, 1 - c, lo, z)
     to_xp, to_xm = at(hi, xp, c, lo, z), at(hi, xm, c, lo, z)
     same, cross = at(hi, x, c, 1 - lo, z), at(1 - hi, x, c, 1 - lo, z)
+    cross_xp, cross_xm = at(1 - hi, xp, c, 1 - lo, z), at(1 - hi, xm, c, 1 - lo, z)
     to_zp, to_zm = at(hi, x, c, lo, lax.rem(z + 1, 16)), at(hi, x, c, lo, lax.rem(z + 15, 16))
     north, south = lax.rem(lat + 15, 16), lax.rem(lat + 1, 16)
     west, east = lax.rem(lon + 31, 32), lax.rem(lon + 1, 32)
@@ -173,7 +184,7 @@
         load.start()
 
     barrier = pltpu.get_barrier_semaphore()
-    friends = (core, to_xp, to_xm, same, cross, to_zp, to_zm) + back + ahead
+    friends = (core, to_xp, to_xm, same, cross, cross_xp, cross_xm, to_zp, to_zm) + back + ahead
     for friend in friends:
         pl.semaphore_signal(barrier, inc=1, device_id=friend, device_id_type=MESH)
     k_ref[:, WIN:, :] = jnp.zeros((NW, 128 - WIN, C), BF16)
@@ -188,8 +199,12 @@
 
     started = []
 
+    every = slice(None)
+
     def message(i, number, slab, target):
-        ref = weights[i].at[slab]
+        weight, rows, columns = PIECES[i]
+        place = slab[:4] + (every,) * (4 - len(slab)) + (rows, columns if len(slab) < 6 else slab[5])
+        ref = weights[weight].at[place]
         return pltpu.make_async_remote_copy(
             src_ref=ref, dst_ref=ref, send_sem=send_sem.at[i, number], recv_sem=recv_sem.at[i, number],
             device_id=target, device_id_type=MESH,
@@ -203,59 +218,91 @@
     def arrived(i, number, slab):
         message(i, number, slab, core).wait_recv()
 
-    every = slice(None)
-
-    def stage0(i):
+    def left(i):
+        columns = PIECES[i][2]
+        return slice(columns.start, (columns.start + columns.stop) // 2)
+
+    def right(i):
+        columns = PIECES[i][2]
+        return slice((columns.start + columns.stop) // 2, columns.stop)
+
+    def give_cross(i, direct):
+        if direct:
+            send(i, B2P, (hi, x, c, other), cross_xp)
+            send(i, B2M, (hi, x, c, other), cross_xm)
         send(i, A1, (hi, x, c, other), cross)
+
+    def give_ring(i):
         send(i, B1P, (hi, x, c, colour), to_xp)
         send(i, B1M, (hi, x, c, colour), to_xm)
+
+    def give_rest(i):
         send(i, A2, (hi, x, c, colour), cross)
         send(i, D_OWN, (hi, x, c), core)
 
-    def stage1(i):
+    def pass_cross(i, direct):
         arrived(i, A1, (1 - hi, x, c, colour))
-        send(i, B2P, (1 - hi, x, c, colour), to_xp)
-        send(i, B2M, (1 - hi, x, c, colour), to_xm)
-
-    def stage2(i):
-        half = SHAPES[i][1] // 2
+        if not direct:
+            send(i, B2P, (1 - hi, x, c, colour), to_xp)
+            send(i, B2M, (1 - hi, x, c, colour), to_xm)
+
+    def swap_far(i, split):
+        if split:
+            send(i, CS, (every, x2, c, colour, every, left(i)), same)
+            send(i, CX, (every, x2, c, colour, every, right(i)), cross)
+        else:
+            send(i, CS, (every, x2, c, colour), same)
+        send(i, D_X2, (every, x2, c, colour), core)
+
+    def pass_near(i, minus):
         arrived(i, B1P, (hi, xm, c, colour))
         arrived(i, B2P, (1 - hi, xm, c, colour))
-        send(i, B3P, (every, xm, c, colour, every, slice(0, half)), to_xp)
+        send(i, B3P, (every, xm, c, colour, every, left(i)), to_xp)
         arrived(i, B1M, (hi, xp, c, colour))
         arrived(i, B2M, (1 - hi, xp, c, colour))
-        send(i, B3M, (every, xp, c, colour, every, slice(half, 2 * half)), to_xm)
-        send(i, CM, (every, xm, c, colour), to_zm)
+        send(i, B3M, (every, xp, c, colour, every, right(i)), to_xm)
+        send(i, CM, (every, xm, c, colour), minus)
         send(i, CP, (every, xp, c, colour), to_zp)
         send(i, D_XM, (every, xm, c, colour), core)
         send(i, D_XP, (every, xp, c, colour), core)
 
-    def stage3(i):
-        half = SHAPES[i][1] // 2
-        arrived(i, B3P, (every, x2, c, colour, every, slice(0, half)))
-        arrived(i, B3M, (every, x2, c, colour, every, slice(half, 2 * half)))
-        send(i, CS, (every, x2, c, colour), same)
-        send(i, D_X2, (every, x2, c, colour), core)
+    def pass_far(i, split):
+        arrived(i, B3P, (every, x2, c, colour, every, left(i)))
+        arrived(i, B3M, (every, x2, c, colour, every, right(i)))
+        swap_far(i, split)
+
+    def share_cross(i):
         arrived(i, A2, (1 - hi, x, c, other))
         send(i, D_CROSS, (1 - hi, x, c), core)
 
-    def stage4(i):
+    def share_near(i):
         arrived(i, CP, (every, xp, c, other))
         send(i, D_ZP, (every, xp, c, other), core)
         arrived(i, CM, (every, xm, c, other))
         send(i, D_ZM, (every, xm, c, other), core)
-        arrived(i, CS, (every, x2, c, other))
+
+    def share_far(i, split):
+        if split:
+            arrived(i, CS, (every, x2, c, other, every, left(i)))
+            arrived(i, CX, (every, x2, c, other, every, right(i)))
+        else:
+            arrived(i, CS, (every, x2, c, other))
         send(i, D_Z2, (every, x2, c, other), core)
 
-    def stage5(i):
-        d = 1 - c
+    d = 1 - c
+
+    def have_column(i):
         arrived(i, D_OWN, (hi, x, d))
         arrived(i, D_CROSS, (1 - hi, x, d))
+
+    def have_near(i):
         arrived(i, D_XM, (every, xm, d, colour))
         arrived(i, D_XP, (every, xp, d, colour))
-        arrived(i, D_X2, (every, x2, d, colour))
         arrived(i, D_ZP, (every, xp, d, other))
         arrived(i, D_ZM, (every, xm, d, other))
+
+    def have_far(i):
+        arrived(i, D_X2, (every, x2, d, colour))
         arrived(i, D_Z2, (every, x2, d, other))
 
     bounds = ((RIM_EAST, RIM_SOUTH), (RIM_SOUTH, RIM_CORNER), (RIM_CORNER, RIM_END))
@@ -280,40 +327,22 @@
             copy.wait_recv()
         rim32[...] = rim_in[slot].astype(F32)
 
-    stage0(0)
-    pack_rim(tok, rim32, rim_out.at[0])
-    send_rims(0, back)
-    stage0(1)
-    stage1(0)
-    stage1(1)
-    stage0(2)
-    stage2(0)
-    pack_rim(gra, rim32, rim_out.at[1])
-    send_rims(1, back)
-    stage1(2)
-    stage0(3)
-    stage3(0)
-    stage2(1)
-    take_rims(0, back)
-    to_windows(tok, rim32, x_ref)
-    values = x_ref[...]
-    scaled1, inverse1 = normalize(values)
-    sc_ref[...] = scaled1
-    normal1 = scaled1.astype(BF16)
-    stage4(0)
-    stage3(1)
-    stage1(3)
-    stage5(0)
+    def have(i):
+        have_column(i)
+        have_near(i)
+        have_far(i)
 
     def whole(i, cols):
         rows = SHAPES[i][0] * 16
         return weights[i][:, :, :, :, :, cols].reshape(rows, cols.stop - cols.start)
 
-    for n, ref in enumerate((q_ref, k_ref, v_ref)):
-        part = nn(normal1, whole(0, slice(C * n, C * (n + 1))))
-        if n == 0:
-            part = part.astype(BF16).astype(F32) * 0.125
-        ref[:, :WIN, :] = part.reshape(NW, WIN, C).astype(BF16)
+    def project():
+        normal1 = sc_ref[...].astype(BF16)
+        for n, ref in enumerate((q_ref, k_ref, v_ref)):
+            part = nn(normal1, whole(0, slice(C * n, C * (n + 1))))
+            if n == 0:
+                part = part.astype(BF16).astype(F32) * 0.125
+            ref[:, :WIN, :] = part.reshape(NW, WIN, C).astype(BF16)
 
     def attend(w, quad):
         lanes = slice(256 * quad, 256 * (quad + 1))
@@ -324,42 +353,116 @@
         p_ref[2 * w + quad] = probs
         m_ref[w, :, lanes] = head_lanes(nn(probs.astype(BF16), v_ref[w, :, lanes])).astype(BF16)
 
-    service = {1: (stage2, 2), 3: (stage4, 1), 5: (stage3, 2), 7: (stage2, 3), 9: (stage4, 2), 10: (stage3, 3)}
-    for n in range(12):
-        attend(n // 2, n % 2)
-        if n in service:
-            stage, i = service[n]
-            stage(i)
-
-    stage5(1)
+    def feed(row, column, first):
+        start = pl.multiple_of((row * 4 + column) * 256, 256)
+        expand = we[:, :, :, :, :, pl.ds(start, 256)].reshape(C, 256)
+        contract = wc[row, column].reshape(256, C)
+        preact = nn(normal2, expand)
+        grad_act = nt(gradient, contract)
+        phi, tail = gelu_parts(preact)
+        part = nn((preact * phi).astype(BF16), contract)
+        grad_part = nt((grad_act * (phi + tail)).astype(BF16), expand)
+        if first:
+            oacc[...] = part
+            gacc[...] = grad_part
+        else:
+            oacc[...] += part
+            gacc[...] += grad_part
+
+    give_cross(0, False)
+    give_ring(0)
+    give_cross(2, False)
+    give_cross(4, False)
+    give_ring(2)
+    give_cross(1, True)
+    give_rest(0)
+    give_ring(1)
+    pass_cross(0, False)
+    pack_rim(tok, rim32, rim_out.at[0])
+    send_rims(0, back)
+    give_rest(3)
+    give_rest(2)
+    pass_cross(2, False)
+    give_cross(3, False)
+    pass_near(0, to_zm)
+    pass_cross(4, False)
+    pass_cross(1, True)
+    give_rest(4)
+    pass_near(1, same)
+    give_ring(4)
+    give_rest(1)
+    share_cross(0)
+    pass_near(2, to_zm)
+    give_ring(3)
+    share_cross(2)
+    pass_far(0, True)
+    take_rims(0, back)
+    to_windows(tok, rim32, x_ref)
+    scaled1, inverse1 = normalize(x_ref[...])
+    sc_ref[...] = scaled1
+    pass_cross(3, False)
+    share_cross(3)
+    pass_far(1, False)
+    pass_near(4, same)
+    share_cross(4)
+    pack_rim(gra, rim32, rim_out.at[1])
+    send_rims(1, back)
+    share_near(1)
+    share_near(0)
+    share_cross(1)
+    share_far(0, True)
+    pass_far(2, True)
+    share_far(1, False)
+    share_near(2)
+    pass_near(3, to_zm)
+    have(0)
+    project()
+    attend(0, 0)
+    attend(0, 1)
+    attend(1, 0)
+    pass_far(4, False)
+    share_near(4)
+    attend(1, 1)
+    attend(2, 0)
+    attend(2, 1)
+    attend(3, 0)
+    share_far(2, True)
+    attend(3, 1)
+    attend(4, 0)
+    pass_far(3, False)
+    take_rims(1, back)
+    to_windows(gra, rim32, gw_ref)
+    attend(4, 1)
+    attend(5, 0)
+    attend(5, 1)
+    share_near(3)
+    have(1)
     attn = nn(flat(m_ref), whole(1, slice(0, C))).astype(BF16).astype(F32)
     hidden = x_ref[...] + attn
     scaled2, inverse2 = normalize(hidden)
     normal2 = scaled2.astype(BF16)
-    take_rims(1, back)
-    to_windows(gra, rim32, gw_ref)
+    x_ref[...] = hidden
+    have(2)
+    have_column(3)
+    have_column(4)
     gradient = gw_ref[...].astype(BF16)
-    stage4(3)
-    stage5(2)
-    stage5(3)
-
-    chunk = 512
-    for f in range(FF // chunk):
-        expand = whole(2, slice(chunk * f, chunk * (f + 1)))
-        contract = wc[f // 2, 2 * (f % 2) : 2 * (f % 2) + 2].reshape(chunk, C)
-        preact = nn(normal2, expand)
-        grad_act = nt(gradient, contract)
-        phi, tail = gelu_parts(preact)
-        feed = nn((preact * phi).astype(BF16), contract)
-        grad_norm2 = nt((grad_act * (phi + tail)).astype(BF16), expand)
-        if f == 0:
-            oacc[...] = feed
-            gacc[...] = grad_norm2
-        else:
-            oacc[...] += feed
-            gacc[...] += grad_norm2
-
-    from_windows(hidden + oacc[...], o_tile, rim32)
+    feed(hi, x, True)
+    feed(1 - hi, x, False)
+    have_near(3)
+    have_near(4)
+    feed(hi, xp, False)
+    share_far(4, False)
+    share_far(3, False)
+    feed(1 - hi, xp, False)
+    feed(hi, xm, False)
+    feed(1 - hi, xm, False)
+    have_far(3)
+    have_far(4)
+    feed(hi, x2, False)
+    feed(1 - hi, x2, False)
+
+    x_ref[...] += oacc[...]
+    from_windows(x_ref, o_tile, rim32)
     rim_out[2] = rim32[...].astype(BF16)
     send_rims(2, ahead)
 
@@ -381,27 +484,48 @@
         gk_ref[w, :, lanes] = tn(grad_scores, queries)[:WIN].astype(BF16)
         gv_ref[w, :, lanes] = tn(probs.astype(BF16), grad_mixed)[:WIN].astype(BF16)
 
-    for n in range(12):
-        attend_back(n // 2, n % 2)
-
-    grad_normal1 = (
-        nt(flat(gq_ref), whole(0, slice(0, C)))
-        + nt(flat(gk_ref), whole(0, slice(C, 2 * C)))
-        + nt(flat(gv_ref), whole(0, slice(2 * C, 3 * C)))
-    )
-    grad_normal1 = grad_normal1.astype(BF16).astype(F32)
-    x_ref[...] = gh_ref[...] + normalize_back(sc_ref[...], inverse1, grad_normal1)
-    from_windows(x_ref, g_tile, rim32)
+    def finish(windows):
+        def pick(ref):
+            parts = [ref[w].astype(F32) for w in windows]
+            return jnp.concatenate(parts, axis=0)
+
+        def pick_flat(ref):
+            parts = [ref[WIN * w : WIN * (w + 1)] for w in windows]
+            return jnp.concatenate(parts, axis=0)
+
+        grad_normal1 = (
+            nt(pick(gq_ref).astype(BF16), whole(0, slice(0, C)))
+            + nt(pick(gk_ref).astype(BF16), whole(0, slice(C, 2 * C)))
+            + nt(pick(gv_ref).astype(BF16), whole(0, slice(2 * C, 3 * C)))
+        )
+        grad_normal1 = grad_normal1.astype(BF16).astype(F32)
+        inverse = pick_flat(inverse1)
+        result = pick_flat(gh_ref) + normalize_back(pick_flat(sc_ref), inverse, grad_normal1)
+        for n, w in enumerate(windows):
+            x_ref[WIN * w : WIN * (w + 1)] = result[WIN * n : WIN * (n + 1)]
+
+    for w in (1, 3, 4, 5):
+        attend_back(w, 0)
+        attend_back(w, 1)
+    finish((1, 3, 4, 5))
+    from_windows(x_ref, g_tile, rim32, True)
     rim_out[3] = rim32[...].astype(BF16)
     send_rims(3, ahead)
+    for w in (0, 2):
+        attend_back(w, 0)
+        attend_back(w, 1)
+    finish((0, 2))
+    from_windows(x_ref, g_tile, rim32, False)
 
     take_rims(2, ahead)
     place_rim(rim32, o_tile)
     out_ref[...] = o_tile[...].astype(BF16)
+    for copy in started[:-3]:
+        copy.wait_send()
     take_rims(3, ahead)
     place_rim(rim32, g_tile)
     gt_ref[...] = g_tile[...].astype(BF16)
-    for copy in started:
+    for copy in started[-3:]:
         copy.wait_send()
 
 
@@ -425,8 +549,8 @@
         ]
         + [pltpu.VMEM((2, 4, 2, 2, rows // 2, columns), BF16) for rows, columns in SHAPES]
         + [
-            pltpu.SemaphoreType.DMA((4, MESSAGES)),
-            pltpu.SemaphoreType.DMA((4, MESSAGES)),
+            pltpu.SemaphoreType.DMA((len(PIECES), MESSAGES)),
+            pltpu.SemaphoreType.DMA((len(PIECES), MESSAGES)),
             pltpu.SemaphoreType.DMA((6,)),
             pltpu.SemaphoreType.DMA((4, 3)),
             pltpu.SemaphoreType.DMA((4, 3)),

time: 69.4 us -> 60.8 us (0.88); the launches traced: 68.3 us -> 60.4 us
  Pallas kernels: 65 us -> 57.1 us
    pallas_call x1, Pallas kernels: 65 us -> 57.1 us  [shards(): pl.pallas_call(kernel, out_shape=[jax.ShapeDtypeStruct((ROWS, COLS, C), B...]
where the time goes in v2:
time: 60.8 us; the launch traced here: 60.4 us
  Pallas kernels  57.1 us (94%)
  local copies, waits for them, and re-layouts  2.62 us (4%)
  between operations  0.65 us (1%)
    pallas_call x1, Pallas kernels, shards(): pl.pallas_call(kernel, out_shape=[jax.ShapeDtypeStruct((ROWS, COLS, C), B...  57.1 us
    unnamed x4, local copies, waits for them, and re-layouts  2.62 us

profile of v2, /device:TPU:24, one launch (start us, length us, event | category | flops | bytes accessed | tf_op | source)
XLA Modules:
  0.0 60.4 jit_solution(11791035785861295788)
XLA Ops:
  0.6 57.1 %swin_block.1 = (bf16[18,24,512]{2,1,0:T(8,128)(2,1)}, bf16[18,24,512]{2,1,0:T(8,128)(2,1)}) custom-call(bf16[18,24,512]{2,1,0:T(8,128)(2,1)} %tok_h.1, bf16[18,24,512]{2,1,0:T(8,128)(2,1)} %gra_h.1, bf16[2,16,1536]{2,1,0:T(8,128)(2,1)} %bitcast.6, bf16[2,16,512]{2,1,0:T(8,128)(2,1)} %bitcast.7, bf16[2,16,2048]{2,1,0:T(8,128)(2,1)} %bitcast.4, ...), custom_call_target="tpu_custom_call" | custom-call | tf_op jit(solution)/shard_map/swin_block/pallas_call | solution.py:541
  57.8 0.0 copy-start
  57.8 1.9 %copy.10 = bf16[18,24,512]{2,1,0:T(8,128)(2,1)} copy(bf16[18,24,512]{2,1,0:T(8,128)(2,1)} %get-tuple-element.4) | data formatting | bytes 884736
  59.6 0.0 copy-done
  59.6 0.8 %copy.11 = bf16[18,24,512]{2,1,0:T(8,128)(2,1)} copy(bf16[18,24,512]{2,1,0:T(8,128)(2,1)S(1)} %copy-done) | data formatting | bytes 884736
Async XLA Ops:
  57.8 1.9 %copy-start = (bf16[18,24,512]{2,1,0:T(8,128)(2,1)S(1)}, bf16[18,24,512]{2,1,0:T(8,128)(2,1)}, u32[]{:S(2)}) copy-start(bf16[18,24,512]{2,1,0:T(8,128)(2,1)} %get-tuple-element.5) | copy-start | bytes 1327108

commit v3 on v2

--- a/solution.py
+++ b/solution.py
@@ -20,7 +20,7 @@
 BF16 = jnp.bfloat16
 MESH = pl.DeviceIdType.MESH
 
-RIM_EAST, RIM_SOUTH, RIM_CORNER, RIM_END = 0, 96, 160, 192
+RIM_WEST, RIM_SOUTH, RIM_CORNER, RIM_END = 0, 96, 160, 192
 
 SHAPES = ((32, 1536), (32, 512), (32, 2048), (128, 512))
 
@@ -87,24 +87,24 @@
     for j in range(ROWS):
         base = (j // WIN_LAT) * 2 * WIN + (j % WIN_LAT) * WIN_LON
         if j < ROWS - 3:
-            runs.append((base, 12, j + 3, 6, None))
-            runs.append((base + WIN, 6, j + 3, 18, None))
-            runs.append((base + WIN + 6, 6, None, None, RIM_EAST + 6 * j))
+            runs.append((base, 6, None, None, RIM_WEST + 6 * j))
+            runs.append((base + 6, 6, j + 3, 0, None))
+            runs.append((base + WIN, 12, j + 3, 6, None))
         else:
             south = RIM_SOUTH + 18 * (j - 15)
-            runs.append((base, 12, None, None, south))
-            runs.append((base + WIN, 6, None, None, south + 12))
-            runs.append((base + WIN + 6, 6, None, None, RIM_CORNER + 6 * (j - 15)))
+            runs.append((base, 6, None, None, RIM_CORNER + 6 * (j - 15)))
+            runs.append((base + 6, 6, None, None, south))
+            runs.append((base + WIN, 12, None, None, south + 6))
     return runs
 
 
 def pack_rim(tile, rim32, rim):
     for j in range(15):
-        rim32[RIM_EAST + 6 * j : RIM_EAST + 6 * j + 6] = tile[j + 3].astype(F32)[:6]
+        rim32[RIM_WEST + 6 * j : RIM_WEST + 6 * j + 6] = tile[j + 3].astype(F32)[18:]
     for j in range(3):
         row = tile[j].astype(F32)
-        rim32[RIM_SOUTH + 18 * j : RIM_SOUTH + 18 * j + 18] = row[6:]
-        rim32[RIM_CORNER + 6 * j : RIM_CORNER + 6 * j + 6] = row[:6]
+        rim32[RIM_SOUTH + 18 * j : RIM_SOUTH + 18 * j + 18] = row[:18]
+        rim32[RIM_CORNER + 6 * j : RIM_CORNER + 6 * j + 6] = row[18:]
     rim[...] = rim32[...].astype(BF16)
 
 
@@ -118,7 +118,7 @@
 
 def from_windows(values, tile32, rim32, edge=None):
     for start, count, row, col, other in segments():
-        if edge is not None and edge == (start // WIN in (0, 2)):
+        if edge is not None and edge == (start // WIN in (1, 3)):
             continue
         if other is None:
             tile32[row, col : col + count] = values[start : start + count]
@@ -128,10 +128,10 @@
 
 def place_rim(rim32, tile32):
     for j in range(15):
-        tile32[j + 3, :6] = rim32[RIM_EAST + 6 * j : RIM_EAST + 6 * j + 6]
+        tile32[j + 3, 18:] = rim32[RIM_WEST + 6 * j : RIM_WEST + 6 * j + 6]
     for j in range(3):
-        tile32[j, 6:] = rim32[RIM_SOUTH + 18 * j : RIM_SOUTH + 18 * j + 18]
-        tile32[j, :6] = rim32[RIM_CORNER + 6 * j : RIM_CORNER + 6 * j + 6]
+        tile32[j, :18] = rim32[RIM_SOUTH + 18 * j : RIM_SOUTH + 18 * j + 18]
+        tile32[j, 18:] = rim32[RIM_CORNER + 6 * j : RIM_CORNER + 6 * j + 6]
 
 
 def make_bias(flag):
@@ -166,11 +166,11 @@
     to_xp, to_xm = at(hi, xp, c, lo, z), at(hi, xm, c, lo, z)
     same, cross = at(hi, x, c, 1 - lo, z), at(1 - hi, x, c, 1 - lo, z)
     cross_xp, cross_xm = at(1 - hi, xp, c, 1 - lo, z), at(1 - hi, xm, c, 1 - lo, z)
-    to_zp, to_zm = at(hi, x, c, lo, lax.rem(z + 1, 16)), at(hi, x, c, lo, lax.rem(z + 15, 16))
+    pair = at(hi, x, c, lo, z + 1 - 2 * lax.rem(z, 2))
     north, south = lax.rem(lat + 15, 16), lax.rem(lat + 1, 16)
     west, east = lax.rem(lon + 31, 32), lax.rem(lon + 1, 32)
-    back = ((lat, west), (north, lon), (north, west))
-    ahead = ((lat, east), (south, lon), (south, east))
+    ahead = ((lat, east), (north, lon), (north, east))
+    back = ((lat, west), (south, lon), (south, west))
 
     weights = (wq, wp, we, wc)
     loads = [
@@ -184,8 +184,8 @@
         load.start()
 
     barrier = pltpu.get_barrier_semaphore()
-    friends = (core, to_xp, to_xm, same, cross, cross_xp, cross_xm, to_zp, to_zm) + back + ahead
-    for friend in friends:
+    plane = (core, to_xp, to_xm, same, cross, cross_xp, cross_xm, pair, (north, lon), (south, lon))
+    for friend in plane + (back[0], back[2]):
         pl.semaphore_signal(barrier, inc=1, device_id=friend, device_id_type=MESH)
     k_ref[:, WIN:, :] = jnp.zeros((NW, 128 - WIN, C), BF16)
     v_ref[:, WIN:, :] = jnp.zeros((NW, 128 - WIN, C), BF16)
@@ -195,7 +195,7 @@
     for load in loads:
         load.wait()
     rim32[...] = jnp.zeros((RIM_END, C), F32)
-    pl.semaphore_wait(barrier, len(friends))
+    pl.semaphore_wait(barrier, len(plane) + 2)
 
     started = []
 
@@ -262,7 +262,7 @@
         arrived(i, B2M, (1 - hi, xp, c, colour))
         send(i, B3M, (every, xp, c, colour, every, right(i)), to_xm)
         send(i, CM, (every, xm, c, colour), minus)
-        send(i, CP, (every, xp, c, colour), to_zp)
+        send(i, CP, (every, xp, c, colour), pair)
         send(i, D_XM, (every, xm, c, colour), core)
         send(i, D_XP, (every, xp, c, colour), core)
 
@@ -305,7 +305,7 @@
         arrived(i, D_X2, (every, x2, d, colour))
         arrived(i, D_Z2, (every, x2, d, other))
 
-    bounds = ((RIM_EAST, RIM_SOUTH), (RIM_SOUTH, RIM_CORNER), (RIM_CORNER, RIM_END))
+    bounds = ((RIM_WEST, RIM_SOUTH), (RIM_SOUTH, RIM_CORNER), (RIM_CORNER, RIM_END))
 
     def rims(slot, targets):
         return [
@@ -369,90 +369,90 @@
             oacc[...] += part
             gacc[...] += grad_part
 
-    give_cross(0, False)
+    give_cross(0, True)
+    give_cross(1, False)
+    give_cross(2, False)
+    pack_rim(tok, rim32, rim_out.at[0])
+    send_rims(0, ahead)
+    give_ring(1)
+    give_rest(3)
+    give_cross(3, False)
+    give_rest(0)
     give_ring(0)
-    give_cross(2, False)
+    give_ring(2)
+    pack_rim(gra, rim32, rim_out.at[1])
+    send_rims(1, ahead)
+    pass_cross(1, False)
+    give_rest(1)
+    pass_cross(0, True)
+    pass_near(0, same)
     give_cross(4, False)
-    give_ring(2)
-    give_cross(1, True)
-    give_rest(0)
-    give_ring(1)
-    pass_cross(0, False)
-    pack_rim(tok, rim32, rim_out.at[0])
-    send_rims(0, back)
-    give_rest(3)
+    pass_cross(2, False)
+    pass_cross(3, False)
+    give_ring(3)
+    pass_near(1, same)
+    share_cross(3)
+    pass_far(0, True)
+    give_rest(4)
     give_rest(2)
-    pass_cross(2, False)
-    give_cross(3, False)
-    pass_near(0, to_zm)
+    pass_near(2, same)
+    share_cross(1)
+    give_ring(4)
+    share_cross(0)
     pass_cross(4, False)
-    pass_cross(1, True)
-    give_rest(4)
-    pass_near(1, same)
-    give_ring(4)
-    give_rest(1)
-    share_cross(0)
-    pass_near(2, to_zm)
-    give_ring(3)
-    share_cross(2)
-    pass_far(0, True)
-    take_rims(0, back)
+    pass_near(3, pair)
+    share_near(0)
+    share_near(1)
+    share_far(0, True)
+    pass_far(1, False)
+    take_rims(0, ahead)
     to_windows(tok, rim32, x_ref)
     scaled1, inverse1 = normalize(x_ref[...])
     sc_ref[...] = scaled1
-    pass_cross(3, False)
-    share_cross(3)
-    pass_far(1, False)
-    pass_near(4, same)
     share_cross(4)
-    pack_rim(gra, rim32, rim_out.at[1])
-    send_rims(1, back)
-    share_near(1)
-    share_near(0)
-    share_cross(1)
-    share_far(0, True)
     pass_far(2, True)
-    share_far(1, False)
-    share_near(2)
-    pass_near(3, to_zm)
     have(0)
     project()
+    pass_near(4, same)
     attend(0, 0)
     attend(0, 1)
     attend(1, 0)
-    pass_far(4, False)
-    share_near(4)
     attend(1, 1)
     attend(2, 0)
+    share_cross(2)
     attend(2, 1)
     attend(3, 0)
-    share_far(2, True)
+    share_near(2)
+    share_far(1, False)
+    pass_far(3, False)
+    take_rims(1, ahead)
+    to_windows(gra, rim32, gw_ref)
     attend(3, 1)
     attend(4, 0)
-    pass_far(3, False)
-    take_rims(1, back)
-    to_windows(gra, rim32, gw_ref)
     attend(4, 1)
+    share_far(2, True)
     attend(5, 0)
+    pass_far(4, False)
+    share_near(3)
     attend(5, 1)
-    share_near(3)
     have(1)
     attn = nn(flat(m_ref), whole(1, slice(0, C))).astype(BF16).astype(F32)
     hidden = x_ref[...] + attn
     scaled2, inverse2 = normalize(hidden)
     normal2 = scaled2.astype(BF16)
     x_ref[...] = hidden
+    share_near(4)
     have(2)
     have_column(3)
     have_column(4)
     gradient = gw_ref[...].astype(BF16)
     feed(hi, x, True)
+    share_far(3, False)
     feed(1 - hi, x, False)
     have_near(3)
     have_near(4)
     feed(hi, xp, False)
     share_far(4, False)
-    share_far(3, False)
     feed(1 - hi, xp, False)
     feed(hi, xm, False)
     feed(1 - hi, xm, False)
@@ -464,7 +464,7 @@
     x_ref[...] += oacc[...]
     from_windows(x_ref, o_tile, rim32)
     rim_out[2] = rim32[...].astype(BF16)
-    send_rims(2, ahead)
+    send_rims(2, back)
 
     grad_hidden = gw_ref[...] + normalize_back(scaled2, inverse2, gacc[...])
     gh_ref[...] = grad_hidden
@@ -504,25 +504,25 @@
         for n, w in enumerate(windows):
             x_ref[WIN * w : WIN * (w + 1)] = result[WIN * n : WIN * (n + 1)]
 
-    for w in (1, 3, 4, 5):
+    for w in (0, 2, 4, 5):
         attend_back(w, 0)
         attend_back(w, 1)
-    finish((1, 3, 4, 5))
+    finish((0, 2, 4, 5))
     from_windows(x_ref, g_tile, rim32, True)
     rim_out[3] = rim32[...].astype(BF16)
-    send_rims(3, ahead)
-    for w in (0, 2):
+    send_rims(3, back)
+    for w in (1, 3):
         attend_back(w, 0)
         attend_back(w, 1)
-    finish((0, 2))
+    finish((1, 3))
     from_windows(x_ref, g_tile, rim32, False)
 
-    take_rims(2, ahead)
+    take_rims(2, back)
     place_rim(rim32, o_tile)
     out_ref[...] = o_tile[...].astype(BF16)
     for copy in started[:-3]:
         copy.wait_send()
-    take_rims(3, ahead)
+    take_rims(3, back)
     place_rim(rim32, g_tile)
     gt_ref[...] = g_tile[...].astype(BF16)
     for copy in started[-3:]:

time: 60.8 us -> 55.3 us (0.910)
  Pallas kernels: 57.1 us -> 51.8 us
    pallas_call x1, Pallas kernels: 57.1 us -> 51.8 us  [shards(): pl.pallas_call(kernel, out_shape=[jax.ShapeDtypeStruct((ROWS, COLS, C), B...]
where the time goes in v3:
time: 55.3 us; the launch traced here: 55.1 us
  Pallas kernels  51.8 us (94%)
  local copies, waits for them, and re-layouts  2.62 us (5%)
  between operations  0.65 us (1%)
    pallas_call x1, Pallas kernels, shards(): pl.pallas_call(kernel, out_shape=[jax.ShapeDtypeStruct((ROWS, COLS, C), B...  51.8 us
    unnamed x4, local copies, waits for them, and re-layouts  2.62 us

profile of v3, /device:TPU:24, one launch (start us, length us, event | category | flops | bytes accessed | tf_op | source)
XLA Modules:
  0.0 55.1 jit_solution(16787119958765123913)
XLA Ops:
  0.6 51.8 %swin_block.1 = (bf16[18,24,512]{2,1,0:T(8,128)(2,1)}, bf16[18,24,512]{2,1,0:T(8,128)(2,1)}) custom-call(bf16[18,24,512]{2,1,0:T(8,128)(2,1)} %tok_h.1, bf16[18,24,512]{2,1,0:T(8,128)(2,1)} %gra_h.1, bf16[2,16,1536]{2,1,0:T(8,128)(2,1)} %bitcast.6, bf16[2,16,512]{2,1,0:T(8,128)(2,1)} %bitcast.7, bf16[2,16,2048]{2,1,0:T(8,128)(2,1)} %bitcast.4, ...), custom_call_target="tpu_custom_call" | custom-call | tf_op jit(solution)/shard_map/swin_block/pallas_call | solution.py:541
  52.5 0.0 copy-start
  52.5 1.9 %copy.10 = bf16[18,24,512]{2,1,0:T(8,128)(2,1)} copy(bf16[18,24,512]{2,1,0:T(8,128)(2,1)} %get-tuple-element.4) | data formatting | bytes 884736
  54.3 0.0 copy-done
  54.3 0.8 %copy.11 = bf16[18,24,512]{2,1,0:T(8,128)(2,1)} copy(bf16[18,24,512]{2,1,0:T(8,128)(2,1)S(1)} %copy-done) | data formatting | bytes 884736
Async XLA Ops:
  52.5 1.9 %copy-start = (bf16[18,24,512]{2,1,0:T(8,128)(2,1)S(1)}, bf16[18,24,512]{2,1,0:T(8,128)(2,1)}, u32[]{:S(2)}) copy-start(bf16[18,24,512]{2,1,0:T(8,128)(2,1)} %get-tuple-element.5) | copy-start | bytes 1327108

commit v4 on v3

--- a/solution.py
+++ b/solution.py
@@ -21,6 +21,7 @@
 MESH = pl.DeviceIdType.MESH
 
 RIM_WEST, RIM_SOUTH, RIM_CORNER, RIM_END = 0, 96, 160, 192
+WEST_EARLY = 64
 
 SHAPES = ((32, 1536), (32, 512), (32, 2048), (128, 512))
 
@@ -116,9 +117,9 @@
             out[start : start + count] = rim32[other : other + count]
 
 
-def from_windows(values, tile32, rim32, edge=None):
+def from_windows(values, tile32, rim32, only=range(NW)):
     for start, count, row, col, other in segments():
-        if edge is not None and edge == (start // WIN in (1, 3)):
+        if start // WIN not in only:
             continue
         if other is None:
             tile32[row, col : col + count] = values[start : start + count]
@@ -166,6 +167,7 @@
     to_xp, to_xm = at(hi, xp, c, lo, z), at(hi, xm, c, lo, z)
     same, cross = at(hi, x, c, 1 - lo, z), at(1 - hi, x, c, 1 - lo, z)
     cross_xp, cross_xm = at(1 - hi, xp, c, 1 - lo, z), at(1 - hi, xm, c, 1 - lo, z)
+    to_x2, cross_x2 = at(hi, x2, c, lo, z), at(1 - hi, x2, c, 1 - lo, z)
     pair = at(hi, x, c, lo, z + 1 - 2 * lax.rem(z, 2))
     north, south = lax.rem(lat + 15, 16), lax.rem(lat + 1, 16)
     west, east = lax.rem(lon + 31, 32), lax.rem(lon + 1, 32)
@@ -184,7 +186,8 @@
         load.start()
 
     barrier = pltpu.get_barrier_semaphore()
-    plane = (core, to_xp, to_xm, same, cross, cross_xp, cross_xm, pair, (north, lon), (south, lon))
+    plane = (core, to_xp, to_xm, to_x2, same, cross, cross_xp, cross_xm, cross_x2)
+    plane += (pair, (north, lon), (south, lon))
     for friend in plane + (back[0], back[2]):
         pl.semaphore_signal(barrier, inc=1, device_id=friend, device_id_type=MESH)
     k_ref[:, WIN:, :] = jnp.zeros((NW, 128 - WIN, C), BF16)
@@ -226,13 +229,17 @@
         columns = PIECES[i][2]
         return slice((columns.start + columns.stop) // 2, columns.stop)
 
-    def give_cross(i, direct):
+    def give_cross(i, direct, far):
+        if direct and far:
+            send(i, B3M, (hi, x, c, other), cross_x2)
         if direct:
             send(i, B2P, (hi, x, c, other), cross_xp)
             send(i, B2M, (hi, x, c, other), cross_xm)
         send(i, A1, (hi, x, c, other), cross)
 
-    def give_ring(i):
+    def give_ring(i, far):
+        if far:
+            send(i, B3P, (hi, x, c, colour), to_x2)
         send(i, B1P, (hi, x, c, colour), to_xp)
         send(i, B1M, (hi, x, c, colour), to_xm)
 
@@ -240,8 +247,10 @@
         send(i, A2, (hi, x, c, colour), cross)
         send(i, D_OWN, (hi, x, c), core)
 
-    def pass_cross(i, direct):
+    def pass_cross(i, direct, far):
         arrived(i, A1, (1 - hi, x, c, colour))
+        if far and not direct:
+            send(i, B3M, (1 - hi, x, c, colour), to_x2)
         if not direct:
             send(i, B2P, (1 - hi, x, c, colour), to_xp)
             send(i, B2M, (1 - hi, x, c, colour), to_xm)
@@ -254,21 +263,27 @@
             send(i, CS, (every, x2, c, colour), same)
         send(i, D_X2, (every, x2, c, colour), core)
 
-    def pass_near(i, minus):
+    def pass_near(i, minus, far):
         arrived(i, B1P, (hi, xm, c, colour))
         arrived(i, B2P, (1 - hi, xm, c, colour))
-        send(i, B3P, (every, xm, c, colour, every, left(i)), to_xp)
+        if not far:
+            send(i, B3P, (every, xm, c, colour, every, left(i)), to_xp)
         arrived(i, B1M, (hi, xp, c, colour))
         arrived(i, B2M, (1 - hi, xp, c, colour))
-        send(i, B3M, (every, xp, c, colour, every, right(i)), to_xm)
+        if not far:
+            send(i, B3M, (every, xp, c, colour, every, right(i)), to_xm)
         send(i, CM, (every, xm, c, colour), minus)
         send(i, CP, (every, xp, c, colour), pair)
         send(i, D_XM, (every, xm, c, colour), core)
         send(i, D_XP, (every, xp, c, colour), core)
 
-    def pass_far(i, split):
-        arrived(i, B3P, (every, x2, c, colour, every, left(i)))
-        arrived(i, B3M, (every, x2, c, colour, every, right(i)))
+    def pass_far(i, split, far):
+        if far:
+            arrived(i, B3P, (hi, x2, c, colour))
+            arrived(i, B3M, (1 - hi, x2, c, colour))
+        else:
+            arrived(i, B3P, (every, x2, c, colour, every, left(i)))
+            arrived(i, B3M, (every, x2, c, colour, every, right(i)))
         swap_far(i, split)
 
     def share_cross(i):
@@ -305,7 +320,9 @@
         arrived(i, D_X2, (every, x2, d, colour))
         arrived(i, D_Z2, (every, x2, d, other))
 
-    bounds = ((RIM_WEST, RIM_SOUTH), (RIM_SOUTH, RIM_CORNER), (RIM_CORNER, RIM_END))
+    bounds = (
+        (RIM_WEST, WEST_EARLY), (WEST_EARLY, RIM_SOUTH), (RIM_SOUTH, RIM_CORNER), (RIM_CORNER, RIM_END),
+    )
 
     def rims(slot, targets):
         return [
@@ -314,7 +331,7 @@
                 send_sem=rim_send_sem.at[slot, n], recv_sem=rim_recv_sem.at[slot, n],
                 device_id=target, device_id_type=MESH,
             )
-            for n, ((a, b), target) in enumerate(zip(bounds, targets))
+            for n, ((a, b), target) in enumerate(zip(bounds, (targets[0],) + targets))
         ]
 
     def send_rims(slot, targets):
@@ -369,51 +386,51 @@
             oacc[...] += part
             gacc[...] += grad_part
 
-    give_cross(0, True)
-    give_cross(1, False)
-    give_cross(2, False)
+    give_cross(0, True, False)
+    give_cross(1, False, False)
+    give_cross(2, False, False)
     pack_rim(tok, rim32, rim_out.at[0])
     send_rims(0, ahead)
-    give_ring(1)
+    give_ring(1, False)
     give_rest(3)
-    give_cross(3, False)
+    give_cross(3, False, False)
     give_rest(0)
-    give_ring(0)
-    give_ring(2)
+    give_ring(0, False)
+    give_ring(2, False)
     pack_rim(gra, rim32, rim_out.at[1])
     send_rims(1, ahead)
-    pass_cross(1, False)
+    pass_cross(1, False, False)
     give_rest(1)
-    pass_cross(0, True)
-    pass_near(0, same)
-    give_cross(4, False)
-    pass_cross(2, False)
-    pass_cross(3, False)
-    give_ring(3)
-    pass_near(1, same)
+    pass_cross(0, True, False)
+    pass_near(0, same, False)
+    give_cross(4, False, False)
+    pass_cross(2, False, False)
+    pass_cross(3, False, False)
+    give_ring(3, False)
+    pass_near(1, same, False)
     share_cross(3)
-    pass_far(0, True)
+    pass_far(0, True, False)
     give_rest(4)
     give_rest(2)
-    pass_near(2, same)
+    pass_near(2, same, False)
     share_cross(1)
-    give_ring(4)
+    give_ring(4, False)
     share_cross(0)
-    pass_cross(4, False)
-    pass_near(3, pair)
+    pass_cross(4, False, False)
+    pass_near(3, pair, False)
     share_near(0)
     share_near(1)
     share_far(0, True)
-    pass_far(1, False)
+    pass_far(1, False, False)
     take_rims(0, ahead)
     to_windows(tok, rim32, x_ref)
     scaled1, inverse1 = normalize(x_ref[...])
     sc_ref[...] = scaled1
     share_cross(4)
-    pass_far(2, True)
+    pass_far(2, True, False)
     have(0)
     project()
-    pass_near(4, same)
+    pass_near(4, same, False)
     attend(0, 0)
     attend(0, 1)
     attend(1, 0)
@@ -424,7 +441,7 @@
     attend(3, 0)
     share_near(2)
     share_far(1, False)
-    pass_far(3, False)
+    pass_far(3, False, False)
     take_rims(1, ahead)
     to_windows(gra, rim32, gw_ref)
     attend(3, 1)
@@ -432,7 +449,7 @@
     attend(4, 1)
     share_far(2, True)
     attend(5, 0)
-    pass_far(4, False)
+    pass_far(4, False, False)
     share_near(3)
     attend(5, 1)
     have(1)
@@ -504,28 +521,34 @@
         for n, w in enumerate(windows):
             x_ref[WIN * w : WIN * (w + 1)] = result[WIN * n : WIN * (n + 1)]
 
-    for w in (0, 2, 4, 5):
-        attend_back(w, 0)
-        attend_back(w, 1)
-    finish((0, 2, 4, 5))
-    from_windows(x_ref, g_tile, rim32, True)
-    rim_out[3] = rim32[...].astype(BF16)
-    send_rims(3, back)
-    for w in (1, 3):
-        attend_back(w, 0)
-        attend_back(w, 1)
-    finish((1, 3))
-    from_windows(x_ref, g_tile, rim32, False)
+    def back_windows(windows):
+        for w in windows:
+            attend_back(w, 0)
+            attend_back(w, 1)
+        finish(windows)
+        from_windows(x_ref, g_tile, rim32, windows)
+
+    back_windows((0, 2))
+    first, second, third, fourth = rims(3, back)
+    rim_out[3, :WEST_EARLY] = rim32[:WEST_EARLY].astype(BF16)
+    first.start()
+    back_windows((4, 5))
+    rim_out[3, WEST_EARLY:] = rim32[WEST_EARLY:].astype(BF16)
+    second.start()
+    third.start()
+    fourth.start()
+    started.extend((first, second, third, fourth))
+    back_windows((1, 3))
 
     take_rims(2, back)
     place_rim(rim32, o_tile)
     out_ref[...] = o_tile[...].astype(BF16)
-    for copy in started[:-3]:
+    for copy in started[:-4]:
         copy.wait_send()
     take_rims(3, back)
     place_rim(rim32, g_tile)
     gt_ref[...] = g_tile[...].astype(BF16)
-    for copy in started[-3:]:
+    for copy in started[-4:]:
         copy.wait_send()
 
 
@@ -540,7 +563,7 @@
     vmem = pl.BlockSpec(memory_space=pltpu.VMEM)
     return pl.pallas_call(
         kernel,
-        out_shape=[jax.ShapeDtypeStruct((ROWS, COLS, C), BF16)] * 2,
+        out_shape=[pltpu.VMEM((ROWS, COLS, C), BF16)] * 2,
         in_specs=[anywhere] * 6,
         out_specs=[vmem] * 2,
         scratch_shapes=[
@@ -552,8 +575,8 @@
             pltpu.SemaphoreType.DMA((len(PIECES), MESSAGES)),
             pltpu.SemaphoreType.DMA((len(PIECES), MESSAGES)),
             pltpu.SemaphoreType.DMA((6,)),
-            pltpu.SemaphoreType.DMA((4, 3)),
-            pltpu.SemaphoreType.DMA((4, 3)),
+            pltpu.SemaphoreType.DMA((4, 4)),
+            pltpu.SemaphoreType.DMA((4, 4)),
             pltpu.VMEM((RIM_END, C), F32),
             pltpu.VMEM((4, RIM_END, C), BF16),
             pltpu.VMEM((4, RIM_END, C), BF16),

time: 55.3 us -> 52.6 us (0.951)
  Pallas kernels: 51.8 us -> 50 us
  local copies, waits for them, and re-layouts: 2.62 us -> 1.53 us
    pallas_call x1, Pallas kernels: 51.8 us -> 50 us  [shards(): pl.pallas_call(kernel, out_shape=[pltpu.VMEM((ROWS, COLS, C), BF16)] * 2,...]
    unnamed x4 -> x2, local copies, waits for them, and re-layouts: 2.62 us -> 1.53 us
where the time goes in v4:
time: 52.6 us; the launch traced here: 52.2 us
  Pallas kernels  50 us (95%)
  local copies, waits for them, and re-layouts  1.53 us (3%)
  between operations  0.64 us (1%)
    pallas_call x1, Pallas kernels, shards(): pl.pallas_call(kernel, out_shape=[pltpu.VMEM((ROWS, COLS, C), BF16)] * 2,...  50 us
    unnamed x2, local copies, waits for them, and re-layouts  1.53 us

profile of v4, /device:TPU:24, one launch (start us, length us, event | category | flops | bytes accessed | tf_op | source)
XLA Modules:
  0.0 52.2 jit_solution(8472073715343639117)
XLA Ops:
  0.6 50.0 %swin_block.1 = (bf16[18,24,512]{2,1,0:T(8,128)(2,1)S(1)}, bf16[18,24,512]{2,1,0:T(8,128)(2,1)S(1)}) custom-call(bf16[18,24,512]{2,1,0:T(8,128)(2,1)} %tok_h.1, bf16[18,24,512]{2,1,0:T(8,128)(2,1)} %gra_h.1, bf16[2,16,1536]{2,1,0:T(8,128)(2,1)} %bitcast.6, bf16[2,16,512]{2,1,0:T(8,128)(2,1)} %bitcast.7, bf16[2,16,2048]{2,1,0:T(8,128)(2,1)} %bitcast.4, ...), custom_call_target="tpu_custom_call" | custom-call | tf_op jit(solution)/shard_map/swin_block/pallas_call | solution.py:564
  50.7 0.8 %copy.10 = bf16[18,24,512]{2,1,0:T(8,128)(2,1)} copy(bf16[18,24,512]{2,1,0:T(8,128)(2,1)S(1)} %get-tuple-element.2) | data formatting | bytes 884736
  51.4 0.8 %copy.11 = bf16[18,24,512]{2,1,0:T(8,128)(2,1)} copy(bf16[18,24,512]{2,1,0:T(8,128)(2,1)S(1)} %get-tuple-element.3) | data formatting | bytes 884736

commit v5 on v4

--- a/solution.py
+++ b/solution.py
@@ -198,6 +198,7 @@
     for load in loads:
         load.wait()
     rim32[...] = jnp.zeros((RIM_END, C), F32)
+    pack_rim(tok, rim32, rim_out.at[0])
     pl.semaphore_wait(barrier, len(plane) + 2)
 
     started = []
@@ -386,11 +387,10 @@
             oacc[...] += part
             gacc[...] += grad_part
 
+    send_rims(0, ahead)
     give_cross(0, True, False)
     give_cross(1, False, False)
     give_cross(2, False, False)
-    pack_rim(tok, rim32, rim_out.at[0])
-    send_rims(0, ahead)
     give_ring(1, False)
     give_rest(3)
     give_cross(3, False, False)
@@ -488,18 +488,19 @@
     proj = whole(1, slice(0, C))
     m_ref[...] = nt(grad_hidden.astype(BF16), proj).reshape(NW, WIN, C).astype(BF16)
 
-    def attend_back(w, quad):
-        lanes = slice(256 * quad, 256 * (quad + 1))
-        grad_mixed = head_rows(m_ref[w, :, lanes].astype(F32))
-        queries = head_rows(q_ref[w, :, lanes].astype(F32))
-        probs = p_ref[2 * w + quad]
-        grad_probs = nt(grad_mixed, v_ref[w, :, lanes])
-        grad_scores = probs * (grad_probs - jnp.sum(grad_probs * probs, axis=-1, keepdims=True))
-        grad_scores = grad_scores.astype(BF16)
-        grad_queries = head_lanes(nn(grad_scores, k_ref[w, :, lanes])) * 0.125
-        gq_ref[w, :, lanes] = grad_queries.astype(BF16)
-        gk_ref[w, :, lanes] = tn(grad_scores, queries)[:WIN].astype(BF16)
-        gv_ref[w, :, lanes] = tn(probs.astype(BF16), grad_mixed)[:WIN].astype(BF16)
+    def attend_back(windows):
+        units = [(w, n, slice(256 * n, 256 * (n + 1))) for w in windows for n in range(2)]
+        grad_mixed = [head_rows(m_ref[w, :, lanes].astype(F32)) for w, _, lanes in units]
+        queries = [head_rows(q_ref[w, :, lanes].astype(F32)) for w, _, lanes in units]
+        probs = [p_ref[2 * w + n] for w, n, _ in units]
+        grad_probs = [nt(part, v_ref[w, :, lanes]) for part, (w, _, lanes) in zip(grad_mixed, units)]
+        grad_values = [tn(p.astype(BF16), part)[:WIN] for p, part in zip(probs, grad_mixed)]
+        inner = [jnp.sum(part * p, axis=-1, keepdims=True) for part, p in zip(grad_probs, probs)]
+        grad_scores = [(p * (part - s)).astype(BF16) for p, part, s in zip(probs, grad_probs, inner)]
+        for part, query, value, (w, _, lanes) in zip(grad_scores, queries, grad_values, units):
+            gq_ref[w, :, lanes] = (head_lanes(nn(part, k_ref[w, :, lanes])) * 0.125).astype(BF16)
+            gk_ref[w, :, lanes] = tn(part, query)[:WIN].astype(BF16)
+            gv_ref[w, :, lanes] = value.astype(BF16)
 
     def finish(windows):
         def pick(ref):
@@ -522,9 +523,7 @@
             x_ref[WIN * w : WIN * (w + 1)] = result[WIN * n : WIN * (n + 1)]
 
     def back_windows(windows):
-        for w in windows:
-            attend_back(w, 0)
-            attend_back(w, 1)
+        attend_back(windows)
         finish(windows)
         from_windows(x_ref, g_tile, rim32, windows)
 

time: 52.6 us -> 50.5 us (0.960)
  the two profiles are of different devices: /device:TPU:24 before, /device:TPU:224 now
where the time goes in v5:
time: 50.5 us; the launch traced here: 50.3 us
  Pallas kernels  48.2 us (95%)
  local copies, waits for them, and re-layouts  1.53 us (3%)
  between operations  0.64 us (1%)
    pallas_call x1, Pallas kernels, shards(): pl.pallas_call(kernel, out_shape=[pltpu.VMEM((ROWS, COLS, C), BF16)] * 2,...  48.2 us
    unnamed x2, local copies, waits for them, and re-layouts  1.53 us

profile of v5, /device:TPU:224, one launch (start us, length us, event | category | flops | bytes accessed | tf_op | source)
XLA Modules:
  0.0 50.3 jit_solution(16735504718581564760)
XLA Ops:
  0.6 48.2 %swin_block.1 = (bf16[18,24,512]{2,1,0:T(8,128)(2,1)S(1)}, bf16[18,24,512]{2,1,0:T(8,128)(2,1)S(1)}) custom-call(bf16[18,24,512]{2,1,0:T(8,128)(2,1)} %tok_h.1, bf16[18,24,512]{2,1,0:T(8,128)(2,1)} %gra_h.1, bf16[2,16,1536]{2,1,0:T(8,128)(2,1)} %bitcast.6, bf16[2,16,512]{2,1,0:T(8,128)(2,1)} %bitcast.7, bf16[2,16,2048]{2,1,0:T(8,128)(2,1)} %bitcast.4, ...), custom_call_target="tpu_custom_call" | custom-call | tf_op jit(solution)/shard_map/swin_block/pallas_call | solution.py:563
  48.8 0.8 %copy.10 = bf16[18,24,512]{2,1,0:T(8,128)(2,1)} copy(bf16[18,24,512]{2,1,0:T(8,128)(2,1)S(1)} %get-tuple-element.2) | data formatting | bytes 884736
  49.6 0.8 %copy.11 = bf16[18,24,512]{2,1,0:T(8,128)(2,1)} copy(bf16[18,24,512]{2,1,0:T(8,128)(2,1)S(1)} %get-tuple-element.3) | data formatting | bytes 884736
